TPU v7x, 128 devices: a whole 4x4x4 slice. The times are simulated.
128 devices in a mesh: gx: 8 (over z_lo, y), gy: 8 (over z_hi, x), grid: 2 (over core).
Axes of the slice: x: 4, y: 4, z: 4 (z_hi: 2, z_lo: 2; z = z_hi * 2 + z_lo), core: 2. Of those that a mesh axis runs over, the one named last changes fastest.
Arguments:
- fine_now: float32 [3, 16, 512, 4096], P(None, 'grid', 'gx', 'gy'), may hold values from -6 to 6
- fine_prev: float32 [3, 16, 512, 4096], P(None, 'grid', 'gx', 'gy'), may hold values from -6 to 6
- fine_mu: float32 [16, 512, 4096], P('grid', 'gx', 'gy'), may hold values from 0.3 to 1
- fine_lam: float32 [16, 512, 4096], P('grid', 'gx', 'gy'), may hold values from 0.3 to 1
- fine_rho: float32 [16, 512, 4096], P('grid', 'gx', 'gy'), may hold values from 1 to 2
- fine_stretch: float32 [16, 512, 4096], P('grid', 'gx', 'gy'), may hold values from 0.7 to 1.4
- coarse_now: float32 [3, 16, 256, 2048], P(None, 'grid', 'gx', 'gy'), may hold values from -6 to 6
- coarse_prev: float32 [3, 16, 256, 2048], P(None, 'grid', 'gx', 'gy'), may hold values from -6 to 6
- coarse_mu: float32 [16, 256, 2048], P('grid', 'gx', 'gy'), may hold values from 1.5 to 4
- coarse_lam: float32 [16, 256, 2048], P('grid', 'gx', 'gy'), may hold values from 1 to 4
- coarse_rho: float32 [16, 256, 2048], P('grid', 'gx', 'gy'), may hold values from 1 to 2
- fine_ghost: float32 [3, 512, 4096], P(None, 'gx', 'gy'), may hold values from -6 to 6
- coarse_ghost: float32 [3, 256, 2048], P(None, 'gx', 'gy'), may hold values from -6 to 6
Outputs:
- fine_next: float32 [3, 16, 512, 4096], P(None, 'grid', 'gx', 'gy')
- coarse_next: float32 [3, 16, 256, 2048], P(None, 'grid', 'gx', 'gy')
All inputs are finite; a program needn't handle non-finite values.
Results may differ from a plain program's by a relative error of at most 0.00002.
Values sent between devices are 32-bit elements; how exact they have to be, the bound alone decides.
No kernel may reach another device: no remote copies, remote signals or barrier semaphores. Data moves between devices by JAX's collectives and lax.ppermute only.
A program may use at most 128 MiB of HBM per device.

v0:
```python
import functools

import jax
import jax.numpy as jnp
import numpy as np
from jax import lax
from jax.experimental import pallas as pl
from jax.experimental.pallas import tpu as pltpu
from jax.sharding import PartitionSpec as P

DT2 = 0.09
DT4 = 0.09 * 0.09 / 12.0
LANES = 128
C1, C2 = 4, 5
HIGHEST = lax.Precision.HIGHEST


def derivative_matrix():
    w = np.zeros((256, 256), np.float32)
    first = {-2: 1.0, -1: -8.0, 1: 8.0, 2: -1.0}
    second = {-2: -1.0, -1: 16.0, 0: -30.0, 1: 16.0, 2: -1.0}
    for lane in range(LANES):
        for base, weights in ((0, first), (LANES, second)):
            for offset, weight in weights.items():
                source = lane + offset
                row = source if 0 <= source < LANES else LANES + source % LANES
                w[row, base + lane] += weight
    return w


def diff1(f):
    return 8.0 * (f(1) - f(-1)) - (f(2) - f(-2))


def diff2(f, centre30):
    return 16.0 * (f(1) + f(-1)) - (f(2) + f(-2)) - centre30


def near_base(g):
    return 4 * (1 - g)


def wave_kernel(
    rows, tiles, stretched, edge_k, block0, block_z, *refs,
):
    (now_hbm, coef_hbm, stretch_hbm, znow_hbm, zcoef_hbm, side_hbm, zside_hbm,
     low_ref, up_ref, zlow_ref, zup_ref, prev_ref, prev4_ref, w_ref,
     step_ref, edge_ref, now, acc, coef, dy, dyy, bb, ee, lhs, sem) = refs
    g = lax.axis_index("grid")
    gx = lax.axis_index("gx")
    ext = rows + 16
    n_coef = 3 if stretched else 2
    own, own_c = 2 + 4 * g, 4 * g
    zed, zed_c = 10 - 8 * g, 8 - 6 * g
    core = pl.ds(8, rows)
    copies = []

    def fetch(src, dst):
        copies.append(pltpu.make_async_copy(src, dst, sem.at[len(copies)]))

    for t in range(tiles):
        lanes = pl.ds(t * LANES, LANES)
        fetch(now_hbm.at[:, :, :, lanes], now.at[:, pl.ds(own, 8), t, core])
        fetch(coef_hbm.at[:, :, :, lanes], coef.at[pl.ds(0, 2), pl.ds(own_c, 8), t, core])
        fetch(znow_hbm.at[:, :, :, lanes], now.at[:, pl.ds(zed, 4), t, core])
        fetch(zcoef_hbm.at[:, :, :, lanes], coef.at[:, pl.ds(zed_c, 2), t, core])
        if stretched:
            fetch(stretch_hbm.at[:, :, lanes], coef.at[2, pl.ds(own_c, 8), t, core])
    fetch(side_hbm.at[pl.ds(0, 3)], now.at[:, pl.ds(own, 8), tiles, core])
    fetch(side_hbm.at[pl.ds(3, n_coef)], coef.at[:, pl.ds(own_c, 8), tiles, core])
    fetch(zside_hbm.at[pl.ds(0, 3)], now.at[:, pl.ds(zed, 4), tiles, core])
    fetch(zside_hbm.at[pl.ds(3, n_coef)], coef.at[:, pl.ds(8 - 8 * g, 4), tiles, core])
    for copy in copies:
        copy.start()
    for field in (now, acc):
        for z in (0, 1, 14, 15):
            field[:, z] = jnp.zeros((3, tiles + 1, ext, LANES), jnp.float32)
    for z in (0, 1, 14, 15):
        dy[:, z] = jnp.zeros((3, ext, LANES), jnp.float32)
        ee[z] = jnp.zeros((ext, LANES), jnp.float32)
    near = near_base(g)
    n_now, width = 6 * (tiles + 1), tiles + 1
    last = lax.axis_size("gx") - 1
    for ref, keep, at_now, at_coef in ((low_ref, gx > 0, 4, 6), (up_ref, gx < last, rows + 8, rows + 8)):
        zref = zlow_ref if ref is low_ref else zup_ref
        groups = ((ref, block0, near), (ref, block0 + block_z, 4 - near), (zref, block0, 8 - 12 * g + 4 * g))
        for source, base, layer in groups:
            first = layer if source is zref else layer + 4 * g
            for t in range(width):
                for c in range(3):
                    for i in range(2):
                        v = jnp.where(keep, source[base + (c * 2 + i) * width + t], 0.0)
                        for h in range(2):
                            now[c, first + 2 + 2 * i + h, t, pl.ds(at_now, 4), :] = v[4 * h : 4 * h + 4]
                for c in range(n_coef):
                    v = jnp.where(keep, source[base + n_now + c * width + t], 0.0)
                    for h in range(4):
                        coef[c, first + h, t, pl.ds(at_coef, 2), :] = v[2 * h : 2 * h + 2]
    for copy in copies:
        copy.wait()

    low_half = lax.broadcasted_iota(jnp.int32, (ext, LANES), 1) < 64

    def y_stage(src, t, z0, chunk):
        after = jnp.where(t == tiles, 0, t + 1)
        before = jnp.where(t == 0, tiles, t - 1)
        n = chunk * 3 * ext
        for k in range(chunk):
            for c in range(3):
                z = z0 + k
                at = pl.ds((k * 3 + c) * ext, ext)
                at_low = pl.ds(n + (k * 3 + c) * ext, ext)
                side = jnp.where(low_half, src[c, z + 2, after], src[c, z + 2, before])
                for h, v in enumerate((src[c, z + 2, t], side)):
                    high = v.astype(jnp.bfloat16)
                    lanes = pl.ds(h * LANES, LANES)
                    lhs[at, lanes] = high
                    lhs[at_low, lanes] = (v - high.astype(jnp.float32)).astype(jnp.bfloat16)
        out = jnp.dot(lhs[pl.ds(0, 2 * n), :], w_ref[...], preferred_element_type=jnp.float32)
        out = out[:n] + out[n:]
        for k in range(chunk):
            for c in range(3):
                r0 = (k * 3 + c) * ext
                dy[c, z0 + k + 2] = out[r0 : r0 + ext, :LANES]
                dyy[c, z0 + k] = out[r0 : r0 + ext, LANES:]

    def mid_stage(src, t, z):
        for r in range(0, ext, 8):
            at = pl.ds(r, 8)
            bb[z, at, :] = diff1(lambda o: src[2, z + 2 + o, t, at, :])
        for r in range(6, ext - 2, 8):
            along = diff1(lambda o: src[0, z + 2, t, pl.ds(r + o, 8), :])
            ee[z + 2, pl.ds(r, 8), :] = along + dy[1, z + 2, pl.ds(r, 8), :]

    def operator(src, t, z, r):
        at = pl.ds(r, 8)
        c1 = coef[0, z, t, at, :]
        c2 = coef[1, z, t, at, :]
        twelfth = 1.0 / 12.0
        laps, xx, zz = [], [], []
        for c in range(3):
            c30 = 30.0 * src[c, z + 2, t, at, :]
            xx.append(diff2(lambda o: src[c, z + 2, t, pl.ds(r + o, 8), :], c30))
            zz.append(diff2(lambda o: src[c, z + 2 + o, t, at, :], c30))
        yy = [dyy[c, z, at, :] for c in range(3)]
        xy_y = diff1(lambda o: dy[1, z + 2, pl.ds(r + o, 8), :])
        xz_z = diff1(lambda o: bb[z, pl.ds(r + o, 8), :])
        xy_x = diff1(lambda o: dy[0, z + 2, pl.ds(r + o, 8), :])
        yz_z = diff1(lambda o: dy[2, z + 2 + o, at, :])
        z_of = diff1(lambda o: ee[z + 2 + o, at, :])
        if stretched:
            s = coef[2, z, t, at, :]
            s2 = s * s
            zz = [s2 * v for v in zz]
            xz_z, yz_z, z_of = s * xz_z, s * yz_z, s * z_of
        laps = [xx[c] + yy[c] + zz[c] for c in range(3)]
        return (
            c1 * laps[0] + c2 * (xx[0] + twelfth * (xy_y + xz_z)),
            c1 * laps[1] + c2 * (yy[1] + twelfth * (xy_x + yz_z)),
            c1 * laps[2] + c2 * (zz[2] + twelfth * z_of),
        )

    def loop(n, f):
        lax.fori_loop(0, n, lambda i, carry: (f(i), carry)[1], 0)

    def first_pass(t):
        loop(12 // C1, lambda i: y_stage(now, t, C1 * i, C1))
        loop(12, lambda z: mid_stage(now, t, z))

        def layer(i):
            z = i + 2 * g
            for r in range(6, ext - 2, 8):
                for c, value in enumerate(operator(now, t, z, r)):
                    acc[c, z + 2, t, pl.ds(r, 8), :] = value

        loop(10, layer)

    loop(tiles + 1, first_pass)

    def finish(t, z, r, previous, store):
        at = pl.ds(r, 8)
        for c, value in enumerate(operator(acc, t, z, r)):
            total = 2.0 * now[c, z + 2, t, at, :] - previous(c) + DT2 * acc[c, z + 2, t, at, :] + DT4 * value
            store(c, total)

    for t in range(tiles + 1):
        loop(10 // C2, lambda i: y_stage(acc, t, C2 * i + 2 * g, C2))
        loop(10, lambda i: mid_stage(acc, t, i + 2 * g))
        if t < tiles:
            lanes = pl.ds(t * LANES, LANES)

            def layer(k):
                z = k + 4 * g
                for r in range(8, rows + 8, 8):
                    at = pl.ds(r - 8, 8)

                    def store(c, value):
                        step_ref[c, k, at, lanes] = value

                    finish(t, z, r, lambda c: prev_ref[c, k, at, lanes], store)

            loop(8, layer)
        else:

            def layer(i):
                z = edge_k + i + 4 * g
                for r in range(8, rows + 8, 8):
                    at = pl.ds(r - 8, 8)

                    def store(c, value):
                        edge_ref[c, i, at, :] = value

                    finish(t, z, r, lambda c: prev4_ref[c, i, at, :], store)

            loop(2, layer)


def wave(now, coef, stretch, znow, zcoef, side, zside, low, up, zlow, zup, prev, prev4, edge_k, block0, block_z):
    rows, cols = prev.shape[2:]
    tiles = cols // LANES
    ext = rows + 16
    stretched = zcoef.shape[0] == 3
    vmem = pl.BlockSpec(memory_space=pltpu.VMEM)
    hbm = pl.BlockSpec(memory_space=pl.ANY)
    f32 = jnp.float32
    units = 3 * (10 * (ext - 8) // 8 * (tiles + 1) + rows * tiles)
    return pl.pallas_call(
        functools.partial(wave_kernel, rows, tiles, stretched, edge_k, block0, block_z),
        out_shape=(
            jax.ShapeDtypeStruct((3, 8, rows, cols), f32),
            jax.ShapeDtypeStruct((3, 2, rows, LANES), f32),
        ),
        in_specs=[hbm] * 7 + [vmem] * 7,
        out_specs=(vmem, vmem),
        scratch_shapes=[
            pltpu.VMEM((3, 16, tiles + 1, ext, LANES), f32),
            pltpu.VMEM((3, 16, tiles + 1, ext, LANES), f32),
            pltpu.VMEM((zcoef.shape[0], 12, tiles + 1, ext, LANES), f32),
            pltpu.VMEM((3, 16, ext, LANES), f32),
            pltpu.VMEM((3, 12, ext, LANES), f32),
            pltpu.VMEM((12, ext, LANES), f32),
            pltpu.VMEM((16, ext, LANES), f32),
            pltpu.VMEM((max(C1, C2) * 6 * ext, 256), jnp.bfloat16),
            pltpu.SemaphoreType.DMA((5 * tiles + 4,)),
        ],
        compiler_params=pltpu.CompilerParams(vmem_limit_bytes=56 * 2**20),
        cost_estimate=pl.CostEstimate(flops=units * 100000, bytes_accessed=10 * 2**20, transcendentals=0),
    )(now, coef, stretch, znow, zcoef, side, zside, low, up, zlow, zup, prev, prev4, jnp.asarray(derivative_matrix(), jnp.bfloat16))


def slots(widths):
    out, tile, lane = [], 0, 0
    for width in widths:
        if lane + width > LANES:
            tile, lane = tile + 1, 0
        out.append((tile, lane))
        lane += width
    return out, tile + 1


FINE_HALO = ((9, 8), (7, 6), (5, 4), (5, 4), (5, 4))
COARSE_HALO = ((7, 8), (5, 6), (3, 4), (3, 4), (3, 4))


def items_of(halo, n_coef):
    kinds = [0] * 24 + [1] * (8 * n_coef) + [2] * 6 + [3] * 3 + [4]
    halos = [halo[k] for k in kinds]
    places, n_tiles = slots([max(h) for h in halos])
    return halos, places, n_tiles


def lane_between(lane, first, width):
    first = first % LANES
    if first + width <= LANES:
        return (lane >= first) & (lane < first + width)
    return (lane >= first) | (lane < first + width - LANES)


def pack_kernel(*refs):
    fine_in, coarse_in, (low_ref, up_ref) = refs[:14], refs[14:26], refs[26:]
    block = 0
    for rows, ins, halo, n_coef in ((64, fine_in, FINE_HALO, 3), (32, coarse_in, COARSE_HALO, 2)):
        halos, places, n_tiles = items_of(halo, n_coef)
        lane = lax.broadcasted_iota(jnp.int32, (rows, LANES), 1)
        half = lane < 64
        pick = lambda i, *at: jnp.where(half, ins[2 * i][at], ins[2 * i + 1][at])
        scale = 12.0 if n_coef == 3 else 48.0

        def coefficients(z):
            mu, lam = pick(1, z), pick(2, z)
            inverse = 1.0 / (scale * pick(3, z))
            out = [mu * inverse, (mu + lam) * inverse]
            return out + [pick(4, z)] if n_coef == 3 else out

        values = [lambda c=c, z=z: pick(0, c, z) for c in range(3) for z in range(8)]
        held = {}

        def coefficient(c, z):
            if z not in held:
                held[z] = coefficients(z)
            return held[z][c]

        values += [lambda c=c, z=z: coefficient(c, z) for z in range(8) for c in range(n_coef)]
        at = 5 if n_coef == 3 else 4
        values += [lambda c=c, z=z: pick(at, c, z) for c in range(3) for z in range(2)]
        values += [lambda c=c: pick(at + 1, c) for c in range(3)]
        if n_coef == 3:
            values.append(lambda: pick(1, 7) * pick(4, 7))
        else:
            values.append(lambda: 2.0 / pick(1, 0))
        for tile in range(n_tiles):
            low = jnp.zeros((rows, LANES), jnp.float32)
            up = jnp.zeros((rows, LANES), jnp.float32)
            for value, (lo, hi), (home, first) in zip(values, halos, places):
                if home == tile:
                    turned = value()
                    turned = pltpu.roll(turned, first, 1) if first else turned
                    low = jnp.where(lane_between(lane, first, hi), turned, low)
                    up = jnp.where(lane_between(lane, first - lo, lo), turned, up)
            for r in range(rows // 8):
                low_ref[block] = low[8 * r : 8 * r + 8]
                up_ref[block] = up[8 * r : 8 * r + 8]
                block += 1


Y_BLOCKS = 8 * items_of(FINE_HALO, 3)[2] + 4 * items_of(COARSE_HALO, 2)[2]


def pack(fine, coarse):
    specs, operands = [], []
    for arrays, layer_of_prev, tiles in ((fine, 3, 4), (coarse, 0, 2)):
        for i, a in enumerate(arrays):
            block = list(a.shape[:-1]) + [LANES]
            at = [0] * a.ndim
            if i == len(arrays) - 2:
                block[1], at[1] = 2, layer_of_prev
            for tile in (0, tiles - 1):
                where = tuple(at[:-1] + [tile])
                specs.append(pl.BlockSpec(tuple(block), lambda i, where=where: where))
                operands.append(a)
    out = jax.ShapeDtypeStruct((Y_BLOCKS, 8, LANES), jnp.float32)
    whole = pl.BlockSpec((Y_BLOCKS, 8, LANES), lambda i: (0, 0, 0))
    return pl.pallas_call(
        pack_kernel, grid=(1,), out_shape=(out, out), in_specs=specs, out_specs=(whole, whole),
        compiler_params=pltpu.CompilerParams(vmem_limit_bytes=56 * 2**20),
    )(*operands)


def coefficient_kernel(scales, *refs):
    n = len(scales)
    for i, scale in enumerate(scales):
        mu, lam, rho = refs[3 * i : 3 * i + 3]
        out = refs[3 * n + i]

        def layer(z, carry, mu=mu, lam=lam, rho=rho, out=out, scale=scale):
            inverse = 1.0 / (scale * rho[z])
            out[0, z] = mu[z] * inverse
            out[1, z] = (mu[z] + lam[z]) * inverse
            return carry

        lax.fori_loop(0, 8, layer, 0)


def coefficients(fine, coarse):
    vmem = pl.BlockSpec(memory_space=pltpu.VMEM)
    outs = tuple(jax.ShapeDtypeStruct((2,) + a[0].shape, jnp.float32) for a in (fine, coarse))
    return pl.pallas_call(
        functools.partial(coefficient_kernel, (12.0, 48.0)), out_shape=outs, in_specs=[vmem] * 6, out_specs=(vmem, vmem),
        compiler_params=pltpu.CompilerParams(vmem_limit_bytes=56 * 2**20),
        cost_estimate=pl.CostEstimate(flops=10**7, bytes_accessed=7 * 2**20, transcendentals=0),
    )(*fine, *coarse)


def unpack_kernel(*refs):
    from_up, from_low = refs[:2]
    fine_edges, coarse_edges = refs[2:8], refs[8:12]
    fine_out, coarse_out, (low_ref, up_ref) = refs[12:16], refs[16:20], refs[20:]
    g = lax.axis_index("grid")
    gy = lax.axis_index("gy")
    keep_low, keep_up = gy > 0, gy < lax.axis_size("gy") - 1
    near = near_base(g)
    block0 = 0
    for rows, halo, n_coef, outs in ((64, FINE_HALO, 3, fine_out), (32, COARSE_HALO, 2, coarse_out)):
        halos, places, n_tiles = items_of(halo, n_coef)
        lane = lax.broadcasted_iota(jnp.int32, (rows, LANES), 1)
        side_ref, prev_ref, ghost_ref, stiff_ref = outs
        stores = [lambda v, c=c, z=z: side_ref.__setitem__((c, z), v) for c in range(3) for z in range(8)]
        stores += [lambda v, c=c, z=z: side_ref.__setitem__((3 + c, z), v) for z in range(8) for c in range(n_coef)]
        stores += [lambda v, c=c, z=z: prev_ref.__setitem__((c, z), v) for c in range(3) for z in range(2)]
        stores += [lambda v, c=c: ghost_ref.__setitem__((c,), v) for c in range(3)]
        stores += [lambda v: stiff_ref.__setitem__((Ellipsis,), v)]
        tiles = []
        for tile in range(n_tiles):
            at = pl.ds(block0 + tile * rows // 8, rows // 8)
            tiles.append((from_up[at].reshape(rows, LANES), from_low[at].reshape(rows, LANES)))
        block0 += n_tiles * rows // 8
        for store, (lo, hi), (home, first) in zip(stores, halos, places):
            up, low = tiles[home]
            both = jnp.where(lane_between(lane, first, hi), up, low)
            both = pltpu.roll(both, LANES - first, 1) if first else both
            valid = ((lane < hi) & keep_up) | ((lane >= LANES - lo) & keep_low)
            store(jnp.where(valid, both, 0.0))
    base, far_base = 0, X_NEAR
    for rows, width, n_coef, outs, edges in ((64, 5, 3, fine_out, fine_edges), (32, 3, 2, coarse_out, coarse_edges)):
        side_ref = outs[0]
        first_rows, last_rows = edges[0::2], edges[1::2]
        for msg, edge, is_last in ((low_ref, first_rows, False), (up_ref, last_rows, True)):
            for start, layer0 in ((base, near), (far_base, 4 - near)):
                for t in range(width):
                    lanes = pl.ds(t * LANES, LANES)

                    def rows_of(kind, c, z, count):
                        if t == width - 1:
                            tile = pl.ds(rows - 8, 8) if is_last else pl.ds(0, 8)
                            v = side_ref[3 * kind + c, z, tile, :]
                        elif kind == 0:
                            v = edge[0][c, z, :, lanes]
                        elif c < 2:
                            v = edge[1][c, z, :, lanes]
                        else:
                            v = edge[2][z, :, lanes]
                        return v[8 - count :] if is_last else v[:count]

                    for c in range(3):
                        for i in range(2):
                            parts = [rows_of(0, c, layer0 + 2 * i + h, 4) for h in range(2)]
                            msg[start + (c * 2 + i) * width + t] = jnp.concatenate(parts, axis=0)
                    for c in range(n_coef):
                        parts = [rows_of(1, c, layer0 + h, 2) for h in range(4)]
                        msg[start + (6 + c) * width + t] = jnp.concatenate(parts, axis=0)
        base += (6 + n_coef) * width
        far_base += (6 + n_coef) * width


X_FINE = 9 * 5
X_NEAR = 9 * 5 + 8 * 3


def unpack(from_up, from_low, fine, coarse):
    vmem = pl.BlockSpec(memory_space=pltpu.VMEM)
    specs, operands = [], []
    whole = pl.BlockSpec((Y_BLOCKS, 8, LANES), lambda i: (0, 0, 0))
    for arrays in (fine, coarse):
        for a in arrays:
            block = list(a.shape)
            block[-2] = 8
            for tile in (0, a.shape[-2] // 8 - 1):
                where = tuple([0] * (a.ndim - 2) + [tile, 0])
                specs.append(pl.BlockSpec(tuple(block), lambda i, where=where: where))
                operands.append(a)
    shapes = []
    for rows, n_coef in ((64, 3), (32, 2)):
        shapes += [(3 + n_coef, 8, rows, LANES), (3, 2, rows, LANES), (3, rows, LANES), (rows, LANES)]
    shapes += [(2 * X_NEAR, 8, LANES)] * 2
    return pl.pallas_call(
        unpack_kernel, grid=(1,),
        out_shape=tuple(jax.ShapeDtypeStruct(s, jnp.float32) for s in shapes),
        in_specs=[whole, whole] + specs,
        out_specs=tuple(pl.BlockSpec(s, lambda i, n=len(s): (0,) * n) for s in shapes),
        compiler_params=pltpu.CompilerParams(vmem_limit_bytes=56 * 2**20),
    )(from_up, from_low, *operands)


def ring(value, axis, by):
    n = lax.axis_size(axis)
    return lax.ppermute(value, axis, [(i, (i + by) % n) for i in range(n)])


def swap(value):
    return lax.ppermute(value, "grid", [(0, 1), (1, 0)])


def neighbours(pieces, axis):
    n = lax.axis_size(axis)
    index = lax.axis_index(axis)
    lows = [lax.slice_in_dim(a, a.shape[d] - lo, a.shape[d], axis=d) for a, d, lo, up in pieces]
    ups = [lax.slice_in_dim(a, 0, up, axis=d) for a, d, lo, up in pieces]

    def move(parts, by, keep):
        flat = jnp.concatenate([p.reshape(-1) for p in parts])
        flat = jnp.pad(flat, (0, -flat.size % 1024)).reshape(-1, LANES)
        flat = jnp.where(keep, ring(flat, axis, by), 0.0).reshape(-1)
        out, at = [], 0
        for p in parts:
            out.append(lax.slice_in_dim(flat, at, at + p.size).reshape(p.shape))
            at += p.size
        return out

    return list(zip(move(lows, 1, index > 0), move(ups, -1, index < n - 1)))


def prolong_matrix(m_rows, m_at, x_rows, x_at):
    out = np.zeros((x_rows, m_rows), np.float32)
    where = {m_at(j): j for j in range(m_rows)}
    for i in range(x_rows):
        x = x_at(i)
        m = x // 2
        weights = {m: 1.0} if x % 2 == 0 else {m - 1: -1 / 16, m: 9 / 16, m + 1: 9 / 16, m + 2: -1 / 16}
        for target, weight in weights.items():
            if target in where:
                out[i, where[target]] = weight
    return out


def restrict_matrix(m_rows, m_at, x_rows, x_at):
    out = np.zeros((m_rows, x_rows), np.float32)
    where = {x_at(i): i for i in range(x_rows)}
    for j in range(m_rows):
        m = m_at(j)
        for target, weight in {2 * m - 1: 0.25, 2 * m: 0.5, 2 * m + 1: 0.25}.items():
            if target in where:
                out[j, where[target]] = weight
    return out


def body(
    fine_now, fine_prev, fine_mu, fine_lam, fine_rho, fine_stretch,
    coarse_now, coarse_prev, coarse_mu, coarse_lam, coarse_rho, fine_ghost, coarse_ghost,
):
    g = lax.axis_index("grid")
    upper = g == 0
    wide = lambda a, b: jnp.concatenate([a, b], axis=-1)
    stiff = fine_mu[7] * fine_stretch[7]
    flex = 2.0 / coarse_mu[0]
    low, up = pack(
        (fine_now, fine_mu, fine_lam, fine_rho, fine_stretch, fine_prev, fine_ghost),
        (coarse_now, coarse_mu, coarse_lam, coarse_rho, coarse_prev, coarse_ghost),
    )
    from_up, from_low = ring(low, "gy", -1), ring(up, "gy", 1)
    fine_coef, coarse_coef = coefficients((fine_mu, fine_lam, fine_rho), (coarse_mu, coarse_lam, coarse_rho))
    cut = lambda a, start, size: lax.dynamic_slice_in_dim(a, start, size, axis=1)
    near = near_base(g)
    near_c = 6 * (1 - g)
    fine_z = swap(cut(fine_now, near, 4)), swap(cut(jnp.concatenate([fine_coef, fine_stretch[None]]), near_c, 2))
    coarse_z = swap(cut(coarse_now, near, 4)), swap(cut(coarse_coef, near_c, 2))
    (fine_side, fine_p4, fine_g4, fine_s4, coarse_side, coarse_p4, coarse_g4, coarse_s4, low, up) = unpack(
        from_up, from_low, (fine_now, fine_coef, fine_stretch), (coarse_now, coarse_coef)
    )
    from_up, from_low = ring(low, "gx", -1), ring(up, "gx", 1)
    fine_zside, coarse_zside = swap(cut(fine_side, near, 4)), swap(cut(coarse_side, near, 4))
    z_up, z_low = swap(from_up[:X_NEAR]), swap(from_low[:X_NEAR])
    msgs = (from_low, from_up, z_low, z_up)
    coarse_step, coarse_edge = wave(
        coarse_now, coarse_coef, coarse_coef[0], *coarse_z, coarse_side, coarse_zside, *msgs, coarse_prev, coarse_p4,
        0, X_FINE, X_NEAR,
    )
    fine_step, fine_edge = wave(
        fine_now, fine_coef, fine_stretch, *fine_z, fine_side, fine_zside, *msgs, fine_prev, fine_p4, 6, 0, X_NEAR
    )

    plane_fine = wide(fine_step[:, 7], fine_edge[:, 1])
    above_fine = wide(fine_step[:, 6], fine_edge[:, 0])
    plane_coarse = wide(coarse_step[:, 0], coarse_edge[:, 0])
    below_coarse = wide(coarse_step[:, 1], coarse_edge[:, 1])
    stiff = wide(stiff, fine_s4)
    flex = wide(flex, coarse_s4)
    fine_planes = jnp.concatenate(
        [plane_fine + above_fine, stiff * (wide(fine_ghost, fine_g4) - above_fine), stiff[None]]
    )
    coarse_planes = jnp.concatenate(
        [plane_coarse + below_coarse, plane_coarse + wide(coarse_ghost, coarse_g4), flex[None]]
    )
    (fl, fu), (cl, cu) = neighbours([(fine_planes, 1, 5, 4), (coarse_planes, 1, 3, 4)], "gx")
    pad = lambda a, n, side: jnp.pad(a, ((0, 0), (n, 0) if side else (0, n), (0, 0)))
    fine_planes = jnp.concatenate([pad(fl, 3, 1), fine_planes, pad(fu, 4, 0)], axis=1)
    coarse_planes = jnp.concatenate([pad(cl, 1, 1), coarse_planes, cu], axis=1)
    fine_other, coarse_other = swap(fine_planes), swap(coarse_planes)
    fine_planes = jnp.where(upper, fine_other, fine_planes)
    coarse_planes = jnp.where(upper, coarse_planes, coarse_other)

    fine_rows, fine_cols = fine_planes.shape[1:]
    coarse_rows, coarse_cols = coarse_planes.shape[1:]
    at_rows = (lambda i: i - 4, lambda i: i - 8)
    cyclic = lambda n: lambda i: i if i < n - LANES // 2 else i - n
    at_cols = (cyclic(coarse_cols), cyclic(fine_cols))
    px = prolong_matrix(coarse_rows, at_rows[0], fine_rows, at_rows[1])
    py = prolong_matrix(coarse_cols, at_cols[0], fine_cols, at_cols[1])
    rx = restrict_matrix(coarse_rows, at_rows[0], fine_rows, at_rows[1])
    ry = restrict_matrix(coarse_cols, at_cols[0], fine_cols, at_cols[1])
    both = lambda mx, my, v: jnp.einsum(
        "ax,nxb->nab", mx, jnp.einsum("nxy,by->nxb", v, my, precision=HIGHEST), precision=HIGHEST
    )
    u, w, s = fine_planes[:3], fine_planes[3:6], fine_planes[6]
    p, q, f = coarse_planes[:3], coarse_planes[3:6], coarse_planes[6]
    start = jnp.where(upper, p - both(rx, ry, w) * f, q)
    end = p - both(rx, ry, s * (both(px, py, start) - u)) * f
    fine_plane = both(px, py, end)[:, 8:-8, :512]
    coarse_plane = end[:, 4:-4, :256]
    fine_out = jnp.where(upper, fine_step[:, 7], fine_plane)
    coarse_out = jnp.where(upper, coarse_plane, coarse_step[:, 0])
    fine_next = jnp.concatenate([fine_step[:, :7], fine_out[:, None]], axis=1)
    coarse_next = jnp.concatenate([coarse_out[:, None], coarse_step[:, 1:]], axis=1)
    return fine_next, coarse_next


def solution(mesh):
    block = P(None, "grid", "gx", "gy")
    scalar = P("grid", "gx", "gy")
    plane = P(None, "gx", "gy")
    return jax.shard_map(
        body,
        mesh=mesh,
        in_specs=(block, block, scalar, scalar, scalar, scalar, block, block, scalar, scalar, scalar, plane, plane),
        out_specs=(block, block),
        check_vma=False,
    )
```

profile of v0, /device:TPU:1, one launch (start us, length us, event | category | flops | bytes accessed | tf_op | source)
XLA Modules:
  0.0 137.1 jit_solution(5798081023563645164)
XLA Ops:
  0.6 4.5 %shard_map.231 = (f32[44,8,128]{2,1,0:T(8,128)}, f32[44,8,128]{2,1,0:T(8,128)}) custom-call(f32[3,8,64,512]{3,2,1,0:T(8,128)} %refs_0_.6, f32[3,8,64,512]{3,2,1,0:T(8,128)} %refs_0_.6, f32[8,64,512]{2,1,0:T(8,128)} %refs_3_.4, f32[8,64,512]{2,1,0:T(8,128)} %refs_3_.4, f32[8,64,512]{2,1,0:T(8,128)} %refs_5_.3, f32[8,64,512]{2,1,0:T(8,128)} %refs_5_.3, ...), custom_call_target="tpu_custom_call" | custom-call | tf_op jit(solution)/shard_map/pallas_call | solution.py:343
  5.1 6.7 %collective-permute-start.2 = (f32[44,8,128]{2,1,0:T(8,128)}, f32[44,8,128]{2,1,0:T(8,128)S(1)}, u32[]{:S(2)}, u32[]{:S(2)}) collective-permute-start(f32[44,8,128]{2,1,0:T(8,128)} %get-tuple-element.21), channel_id=1, source_target_pairs={{0,14},{2,0},{4,2},{6,4},{8,6},{10,8},{12,10},{14,12},{1,15},{3,1}... | collective-permute-start | bytes 540680 | tf_op jit(solution)/shard_map/ppermute | solution.py:466
  11.8 1.4 constant_dynamic-slice_fusion.4
  14.1 3.8 %shard_map.230 = (f32[2,8,64,512]{3,2,1,0:T(8,128)}, f32[2,8,32,256]{3,2,1,0:T(8,128)}) custom-call(f32[8,64,512]{2,1,0:T(8,128)} %refs_3_.4, f32[8,64,512]{2,1,0:T(8,128)} %refs_5_.3, f32[8,64,512]{2,1,0:T(8,128)} %refs_7_.2, f32[8,32,256]{2,1,0:T(8,128)} %refs_17_.1, f32[8,32,256]{2,1,0:T(8,128)} %refs_19_.1, f32[8,32,256]{2,1,0:T(8,128)} %refs_21_.1), custom_call_target="tpu_custom_call" | custom-call | flops 10000000 | bytes 7340032 | tf_op jit(solution)/shard_map/pallas_call | solution.py:367
  17.9 1.6 %constant_dynamic-slice_fusion.1 = f32[2,2,32,256]{3,2,1,0:T(8,128)} fusion(f32[2,8,32,256]{3,2,1,0:T(8,128)} %get-tuple-element.23.refs_10_.refs_11_.refs_1_, s32[]{:T(128)S(6)} %select_n.67), kind=kLoop, calls=%fused_computation.66 | loop fusion | bytes 262148 | tf_op jit(solution)/shard_map/dynamic_slice | solution.py:531
  20.8 1.7 %slice_bitcast_fusion.2.refs_2_ = f32[8,32,256]{2,1,0:T(8,128)} fusion(f32[2,8,32,256]{3,2,1,0:T(8,128)} %get-tuple-element.23.refs_10_.refs_11_.refs_1_), kind=kLoop, calls=%fused_computation.34 | loop fusion | bytes 524288 | tf_op jit(solution)/shard_map/squeeze | solution.py:544
  23.2 4.4 %shard_map.232 = (f32[6,8,64,128]{3,2,1,0:T(8,128)}, f32[3,2,64,128]{3,2,1,0:T(8,128)}, f32[3,64,128]{2,1,0:T(8,128)}, f32[64,128]{1,0:T(8,128)}, f32[5,8,32,128...) custom-call(f32[44,8,128]{2,1,0:T(8,128)} %copy-done.17, ...), custom_call_target="tpu_custom_call" | custom-call | tf_op jit(solution)/shard_map/pallas_call | solution.py:455
  27.6 1.4 collective-permute-start.5
  29.0 2.3 %collective-permute-start.6 = (f32[138,8,128]{2,1,0:T(8,128)}, f32[138,8,128]{2,1,0:T(8,128)}, u32[]{:S(2)}, u32[]{:S(2)}) collective-permute-start(f32[138,8,128]{2,1,0:T(8,128)} %get-tuple-element.26), channel_id=1, source_target_pairs={{0,112},{16,0},{32,16},{48,32},{64,48},{80,64},{96,80},{112,96},{1... | collective-permute-start | bytes 1695752 | tf_op jit(solution)/shard_map/ppermute | solution.py:466
  34.3 10.2 %collective-permute-done.5.refs_7_ = f32[138,8,128]{2,1,0:T(8,128)} collective-permute-done((f32[138,8,128]{2,1,0:T(8,128)}, f32[138,8,128]{2,1,0:T(8,128)}, u32[]{:S(2)}, u32[]{:S(2)}) %collective-permute-start.5) | collective-permute-done | bytes 565280 | tf_op jit(solution)/shard_map/ppermute | solution.py:466
  50.7 14.9 %shard_map.234 = (f32[3,8,32,256]{3,2,1,0:T(8,128)}, f32[3,2,32,128]{3,2,1,0:T(8,128)}) custom-call(f32[3,8,32,256]{3,2,1,0:T(8,128)} %refs_0_.7, f32[2,8,32,256]{3,2,1,0:T(8,128)} %get-tuple-element.23.refs_10_.refs_11_.refs_1_, f32[8,32,256]{2,1,0:T(8,128)} %slice_bitcast_fusion.2.refs_2_, f32[3,4,32,256]{3,2,1,0:T(8,128)} %copy-done.14, ...), custom_call_target="tpu_custom_call" | custom-call | flops 64200000 | bytes 10485760 | tf_op jit(solution)/shard_map/pallas_call | solution.py:227
  68.7 35.8 %shard_map.233 = (f32[3,8,64,512]{3,2,1,0:T(8,128)}, f32[3,2,64,128]{3,2,1,0:T(8,128)}) custom-call(f32[3,8,64,512]{3,2,1,0:T(8,128)} %refs_0_.6, f32[2,8,64,512]{3,2,1,0:T(8,128)} %get-tuple-element.20.refs_4_.refs_5_.refs_1_, f32[8,64,512]{2,1,0:T(8,128)} %refs_2_.7, f32[3,4,64,512]{3,2,1,0:T(8,128)} %collective-permute-done.refs_3_, ...), custom_call_target="tpu_custom_call" | custom-call | flops 211800000 | bytes 10485760 | tf_op jit(solution)/shard_map/pallas_call | solution.py:227
  104.5 1.1 slice_bitcast_fusion
  107.0 2.5 %collective-permute-start.13 = (f32[224,128]{1,0:T(8,128)S(1)}, f32[224,128]{1,0:T(8,128)S(1)}, u32[]{:S(2)}, u32[]{:S(2)}) collective-permute-start(f32[224,128]{1,0:T(8,128)S(1)} %maximum_bitcast_fusion), channel_id=1, source_target_pairs={{0,112},{16,0},{32,16},{48,32},{64,48},{80,64},{96,80},{112,96},{1... | collective-permute-start | bytes 344072 | tf_op jit(solution)/shard_map/ppermute | solution.py:466
  109.6 2.4 %collective-permute-done.13 = f32[224,128]{1,0:T(8,128)S(1)} collective-permute-done((f32[224,128]{1,0:T(8,128)S(1)}, f32[224,128]{1,0:T(8,128)S(1)}, u32[]{:S(2)}, u32[]{:S(2)}) %collective-permute-start.13) | collective-permute-done | bytes 114720 | tf_op jit(solution)/shard_map/ppermute | solution.py:466
  112.1 4.2 %collective-permute-done.12 = f32[240,128]{1,0:T(8,128)S(1)} collective-permute-done((f32[240,128]{1,0:T(8,128)S(1)}, f32[240,128]{1,0:T(8,128)S(1)}, u32[]{:S(2)}, u32[]{:S(2)}) %collective-permute-start.12) | collective-permute-done | bytes 122912 | tf_op jit(solution)/shard_map/ppermute | solution.py:466
  116.3 1.2 select_maximum_fusion
  117.6 1.2 collective-permute-start.15
  119.7 1.2 slice.133
  120.8 2.0 %slice.104 = f32[3,7,64,512]{3,2,1,0:T(8,128)S(1)} slice(f32[3,8,64,512]{3,2,1,0:T(8,128)} %get-tuple-element.28), slice={[0:3], [0:7], [0:64], [0:512]} | slice | bytes 5505024 | tf_op jit(solution)/shard_map/slice | solution.py:591
  122.9 1.1 broadcast_select_fusion.1
  125.2 1.3 fusion.18
  128.7 1.3 fusion.7
  135.1 2.0 %pad_maximum_fusion = f32[3,8,64,512]{3,2,1,0:T(8,128)} fusion(f32[3,1,64,512]{3,2,1,0:T(8,128)S(1)} %fusion.11, f32[3,7,64,512]{3,2,1,0:T(8,128)S(1)} %slice.104), kind=kLoop, calls=%fused_computation.2 | loop fusion | flops 786432 | bytes 6291456 | tf_op jit(solution)/shard_map/concatenate | solution.py:591
  (125 shorter events, 25.9 us)
Async XLA Ops:
  0.6 11.2 %copy-start = (f32[3,8,64,512]{3,2,1,0:T(8,128)S(1)}, f32[3,8,64,512]{3,2,1,0:T(8,128)}, u32[]{:S(2)}) copy-start(f32[3,8,64,512]{3,2,1,0:T(8,128)} %refs_0_.6) | copy-start | bytes 9437188
  5.1 17.4 %collective-permute-start.2 = (f32[44,8,128]{2,1,0:T(8,128)}, f32[44,8,128]{2,1,0:T(8,128)S(1)}, u32[]{:S(2)}, u32[]{:S(2)}) collective-permute-start(f32[44,8,128]{2,1,0:T(8,128)} %get-tuple-element.21), channel_id=1, source_target_pairs={{0,14},{2,0},{4,2},{6,4},{8,6},{10,8},{12,10},{14,12},{1,15},{3,1}... | collective-permute-start | bytes 540680 | tf_op jit(solution)/shard_map/ppermute | solution.py:466
  11.8 10.7 %collective-permute-start.3 = (f32[44,8,128]{2,1,0:T(8,128)}, f32[44,8,128]{2,1,0:T(8,128)S(1)}, u32[]{:S(2)}, u32[]{:S(2)}) collective-permute-start(f32[44,8,128]{2,1,0:T(8,128)} %get-tuple-element.22), channel_id=1, source_target_pairs={{0,2},{2,4},{4,6},{6,8},{8,10},{10,12},{12,14},{14,0},{1,3},{3,5},... | collective-permute-start | bytes 540680 | tf_op jit(solution)/shard_map/ppermute | solution.py:466
  13.1 54.4 %collective-permute-start = (f32[3,4,64,512]{3,2,1,0:T(8,128)}, f32[3,4,64,512]{3,2,1,0:T(8,128)}, u32[]{:S(2)}, u32[]{:S(2)}) collective-permute-start(f32[3,4,64,512]{3,2,1,0:T(8,128)} %constant_dynamic-slice_fusion.4), channel_id=1, source_target_pairs={{0,1},{1,0},{2,3},{3,2},{4,5},{5,4},{6,7},{7,6},{8,9},{9,8},{10,11... | collective-permute-start | bytes 4718600 | tf_op jit(solution)/shard_map/ppermute | solution.py:470
  19.5 27.9 %collective-permute-start.10 = (f32[2,2,32,256]{3,2,1,0:T(8,128)}, f32[2,2,32,256]{3,2,1,0:T(8,128)S(1)}, u32[]{:S(2)}, u32[]{:S(2)}) collective-permute-start(f32[2,2,32,256]{3,2,1,0:T(8,128)} %constant_dynamic-slice_fusion.1), channel_id=1, source_target_pairs={{0,1},{1,0},{2,3},{3,2},{4,5},{5,4},{6,7},{7,6},{8,9},{9,8},{10,11... | collective-permute-start | bytes 393224 | tf_op jit(solution)/shard_map/ppermute | solution.py:470
  20.4 28.6 %collective-permute-start.9 = (f32[3,4,32,256]{3,2,1,0:T(8,128)}, f32[3,4,32,256]{3,2,1,0:T(8,128)S(1)}, u32[]{:S(2)}, u32[]{:S(2)}) collective-permute-start(f32[3,4,32,256]{3,2,1,0:T(8,128)} %constant_dynamic-slice_fusion.2), channel_id=1, source_target_pairs={{0,1},{1,0},{2,3},{3,2},{4,5},{5,4},{6,7},{7,6},{8,9},{9,8},{10,11... | collective-permute-start | bytes 1179656 | tf_op jit(solution)/shard_map/ppermute | solution.py:470
  23.2 8.0 %copy-start.1 = (f32[8,64,512]{2,1,0:T(8,128)S(1)}, f32[8,64,512]{2,1,0:T(8,128)}, u32[]{:S(2)}) copy-start(f32[8,64,512]{2,1,0:T(8,128)} %refs_2_.7) | copy-start | bytes 3145732
  23.2 9.7 %copy-start.2 = (f32[2,8,64,512]{3,2,1,0:T(8,128)S(1)}, f32[2,8,64,512]{3,2,1,0:T(8,128)}, u32[]{:S(2)}) copy-start(f32[2,8,64,512]{3,2,1,0:T(8,128)} %get-tuple-element.20.refs_4_.refs_5_.refs_1_) | copy-start | bytes 6291460
  27.6 16.8 %collective-permute-start.5 = (f32[138,8,128]{2,1,0:T(8,128)}, f32[138,8,128]{2,1,0:T(8,128)}, u32[]{:S(2)}, u32[]{:S(2)}) collective-permute-start(f32[138,8,128]{2,1,0:T(8,128)} %get-tuple-element.25), channel_id=1, source_target_pairs={{0,16},{16,32},{32,48},{48,64},{64,80},{80,96},{96,112},{112,0},{1... | collective-permute-start | bytes 1695752 | tf_op jit(solution)/shard_map/ppermute | solution.py:466
  29.0 17.3 %collective-permute-start.6 = (f32[138,8,128]{2,1,0:T(8,128)}, f32[138,8,128]{2,1,0:T(8,128)}, u32[]{:S(2)}, u32[]{:S(2)}) collective-permute-start(f32[138,8,128]{2,1,0:T(8,128)} %get-tuple-element.26), channel_id=1, source_target_pairs={{0,112},{16,0},{32,16},{48,32},{64,48},{80,64},{96,80},{112,96},{1... | collective-permute-start | bytes 1695752 | tf_op jit(solution)/shard_map/ppermute | solution.py:466
  34.0 14.0 %copy-start.25 = (f32[32,128]{1,0:T(8,128)S(1)}, f32[32,128]{1,0:T(8,128)}, u32[]{:S(2)}) copy-start(f32[32,128]{1,0:T(8,128)} %get-tuple-element.37) | copy-start | bytes 49156
  34.0 14.0 %copy-start.24 = (f32[64,128]{1,0:T(8,128)S(1)}, f32[64,128]{1,0:T(8,128)}, u32[]{:S(2)}) copy-start(f32[64,128]{1,0:T(8,128)} %get-tuple-element.30) | copy-start | bytes 98308
  34.0 14.0 %copy-start.6 = (f32[6,8,64,128]{3,2,1,0:T(8,128)S(1)}, f32[6,8,64,128]{3,2,1,0:T(8,128)}, u32[]{:S(2)}) copy-start(f32[6,8,64,128]{3,2,1,0:T(8,128)} %get-tuple-element.24.refs_5_) | copy-start | bytes 4718596
  44.5 5.3 %collective-permute-start.11 = (f32[5,4,32,128]{3,2,1,0:T(8,128)S(1)}, f32[5,4,32,128]{3,2,1,0:T(8,128)S(1)}, u32[]{:S(2)}, u32[]{:S(2)}) collective-permute-start(f32[5,4,32,128]{3,2,1,0:T(8,128)S(1)} %constant_dynamic-slice_fusion), channel_id=1, source_target_pairs={{0,1},{1,0},{2,3},{3,2},{4,5},{5,4},{6,7},{7,6},{8,9},{9,8},{10,11... | collective-permute-start | bytes 983048 | tf_op jit(solution)/shard_map/ppermute | solution.py:470
  46.3 3.5 %collective-permute-start.7 = (f32[69,8,128]{2,1,0:T(8,128)S(1)}, f32[69,8,128]{2,1,0:T(8,128)S(1)}, u32[]{:S(2)}, u32[]{:S(2)}) collective-permute-start(f32[69,8,128]{2,1,0:T(8,128)S(1)} %slice.134), channel_id=1, source_target_pairs={{0,1},{1,0},{2,3},{3,2},{4,5},{5,4},{6,7},{7,6},{8,9},{9,8},{10,11... | collective-permute-start | bytes 847880 | tf_op jit(solution)/shard_map/ppermute | solution.py:470
  47.4 2.4 %collective-permute-start.8 = (f32[69,8,128]{2,1,0:T(8,128)S(1)}, f32[69,8,128]{2,1,0:T(8,128)S(1)}, u32[]{:S(2)}, u32[]{:S(2)}) collective-permute-start(f32[69,8,128]{2,1,0:T(8,128)S(1)} %slice.135), channel_id=1, source_target_pairs={{0,1},{1,0},{2,3},{3,2},{4,5},{5,4},{6,7},{7,6},{8,9},{9,8},{10,11... | collective-permute-start | bytes 847880 | tf_op jit(solution)/shard_map/ppermute | solution.py:470
  49.0 18.5 %collective-permute-start.1 = (f32[3,2,64,512]{3,2,1,0:T(8,128)}, f32[3,2,64,512]{3,2,1,0:T(8,128)S(1)}, u32[]{:S(2)}, u32[]{:S(2)}) collective-permute-start(f32[3,2,64,512]{3,2,1,0:T(8,128)} %fusion.5), channel_id=1, source_target_pairs={{0,1},{1,0},{2,3},{3,2},{4,5},{5,4},{6,7},{7,6},{8,9},{9,8},{10,11... | collective-permute-start | bytes 2359304 | tf_op jit(solution)/shard_map/ppermute | solution.py:470
  49.8 17.8 %collective-permute-start.4 = (f32[6,4,64,128]{3,2,1,0:T(8,128)}, f32[6,4,64,128]{3,2,1,0:T(8,128)S(1)}, u32[]{:S(2)}, u32[]{:S(2)}) collective-permute-start(f32[6,4,64,128]{3,2,1,0:T(8,128)} %constant_dynamic-slice_fusion.3), channel_id=1, source_target_pairs={{0,1},{1,0},{2,3},{3,2},{4,5},{5,4},{6,7},{7,6},{8,9},{9,8},{10,11... | collective-permute-start | bytes 2359304 | tf_op jit(solution)/shard_map/ppermute | solution.py:470
  50.7 16.7 %copy-start.11 = (f32[3,32,256]{2,1,0:T(8,128)S(1)}, f32[3,32,256]{2,1,0:T(8,128)}, u32[]{:S(2)}) copy-start(f32[3,32,256]{2,1,0:T(8,128)} %refs_25_.1) | copy-start | bytes 294916
  50.7 16.7 %copy-start.23 = (f32[3,32,128]{2,1,0:T(8,128)S(1)}, f32[3,32,128]{2,1,0:T(8,128)}, u32[]{:S(2)}) copy-start(f32[3,32,128]{2,1,0:T(8,128)} %get-tuple-element.36) | copy-start | bytes 147460
  107.0 5.0 %collective-permute-start.13 = (f32[224,128]{1,0:T(8,128)S(1)}, f32[224,128]{1,0:T(8,128)S(1)}, u32[]{:S(2)}, u32[]{:S(2)}) collective-permute-start(f32[224,128]{1,0:T(8,128)S(1)} %maximum_bitcast_fusion), channel_id=1, source_target_pairs={{0,112},{16,0},{32,16},{48,32},{64,48},{80,64},{96,80},{112,96},{1... | collective-permute-start | bytes 344072 | tf_op jit(solution)/shard_map/ppermute | solution.py:466
  109.6 6.7 %collective-permute-start.12 = (f32[240,128]{1,0:T(8,128)S(1)}, f32[240,128]{1,0:T(8,128)S(1)}, u32[]{:S(2)}, u32[]{:S(2)}) collective-permute-start(f32[240,128]{1,0:T(8,128)S(1)} %fusion.13), channel_id=1, source_target_pairs={{0,16},{16,32},{32,48},{48,64},{64,80},{80,96},{96,112},{112,0},{1... | collective-permute-start | bytes 368648 | tf_op jit(solution)/shard_map/ppermute | solution.py:466
  117.6 6.4 %collective-permute-start.15 = (f32[7,80,640]{2,1,0:T(8,128)}, f32[7,80,640]{2,1,0:T(8,128)S(1)}, u32[]{:S(2)}, u32[]{:S(2)}) collective-permute-start(f32[7,80,640]{2,1,0:T(8,128)} %select_maximum_fusion), channel_id=1, source_target_pairs={{0,1},{1,0},{2,3},{3,2},{4,5},{5,4},{6,7},{7,6},{8,9},{9,8},{10,11... | collective-permute-start | bytes 4300808 | tf_op jit(solution)/shard_map/ppermute | solution.py:470
  119.7 3.2 %collective-permute-start.14 = (f32[7,40,384]{2,1,0:T(8,128)}, f32[7,40,384]{2,1,0:T(8,128)}, u32[]{:S(2)}, u32[]{:S(2)}) collective-permute-start(f32[7,40,384]{2,1,0:T(8,128)} %fusion.10), channel_id=1, source_target_pairs={{0,1},{1,0},{2,3},{3,2},{4,5},{5,4},{6,7},{7,6},{8,9},{9,8},{10,11... | collective-permute-start | bytes 1290248 | tf_op jit(solution)/shard_map/ppermute | solution.py:470
  (18 other events, 29.2 us)
where the time goes:
time: 138 us; the launch traced here: 137 us
  Pallas kernels  63.3 us (46%)
  local copies, waits for them, and re-layouts  20.4 us (15%)
  starting transfers between devices  17.2 us (12%)
  waiting for transfers between devices  16.8 us (12%)
  other arithmetic  11.3 us (8%)
  matrix products  6.87 us (5%)
    pallas_call x2, Pallas kernels, wave(): pl.pallas_call(functools.partial(wave_kernel, rows, tiles, stretched, edg...  50.6 us
    ppermute x6, waiting for transfers between devices, ring(): return lax.ppermute(value, axis, [(i, (i + by) % n) for i in range(n)])  16.8 us
    ppermute x6, starting transfers between devices, ring(): return lax.ppermute(value, axis, [(i, (i + by) % n) for i in range(n)])  12.9 us
    dot_general x4, matrix products, body(): jnp.einsum('nxy,by->nxb', v, my, precision=HIGHEST)  4.81 us
    unnamed x52, local copies, waits for them, and re-layouts  4.71 us
    dynamic_slice x5, local copies, waits for them, and re-layouts, body(): lax.dynamic_slice_in_dim(a, start, size, axis=1)  4.7 us
    pallas_call x1, Pallas kernels, pack(): pl.pallas_call(pack_kernel, grid=(1,), out_shape=(out, out), in_specs=spe...  4.45 us
    pallas_call x1, Pallas kernels, unpack(): pl.pallas_call(unpack_kernel, grid=(1,), out_shape=tuple((jax.ShapeDtypeS...  4.39 us
  transfers between devices with their start and end apart: 16, of which 3 were waited for; matrix products, arithmetic and copies ran while one was open for 13% of the time, Pallas kernels for 17%

commit v1 on v0

--- a/solution.py
+++ b/solution.py
@@ -41,11 +41,11 @@
 
 
 def wave_kernel(
-    rows, tiles, stretched, edge_k, block0, block_z, *refs,
+    rows, tiles, stretched, edge_k, *refs,
 ):
     (now_hbm, coef_hbm, stretch_hbm, znow_hbm, zcoef_hbm, side_hbm, zside_hbm,
-     low_ref, up_ref, zlow_ref, zup_ref, prev_ref, prev4_ref, w_ref,
-     step_ref, edge_ref, now, acc, coef, dy, dyy, bb, ee, lhs, sem) = refs
+     low_ref, up_ref, zlow_ref, zup_ref, prev_hbm, prev4_ref, ghost_ref, ghost4_ref, stiff_ref, stiff4_ref, w_ref,
+     step_hbm, plane_ref, prev_ref, step_ref, edge_ref, now, acc, coef, dy, dyy, bb, ee, lhs, sem, out_sem) = refs
     g = lax.axis_index("grid")
     gx = lax.axis_index("gx")
     ext = rows + 16
@@ -53,24 +53,30 @@
     own, own_c = 2 + 4 * g, 4 * g
     zed, zed_c = 10 - 8 * g, 8 - 6 * g
     core = pl.ds(8, rows)
-    copies = []
-
-    def fetch(src, dst):
-        copies.append(pltpu.make_async_copy(src, dst, sem.at[len(copies)]))
-
-    for t in range(tiles):
-        lanes = pl.ds(t * LANES, LANES)
-        fetch(now_hbm.at[:, :, :, lanes], now.at[:, pl.ds(own, 8), t, core])
-        fetch(coef_hbm.at[:, :, :, lanes], coef.at[pl.ds(0, 2), pl.ds(own_c, 8), t, core])
-        fetch(znow_hbm.at[:, :, :, lanes], now.at[:, pl.ds(zed, 4), t, core])
-        fetch(zcoef_hbm.at[:, :, :, lanes], coef.at[:, pl.ds(zed_c, 2), t, core])
+
+    def fetches(t):
+        lanes = pl.ds(t * LANES, LANES) if isinstance(t, int) else pl.ds(pl.multiple_of(t * LANES, LANES), LANES)
+        pairs = [
+            (now_hbm.at[:, :, :, lanes], now.at[:, pl.ds(own, 8), t, core]),
+            (znow_hbm.at[:, :, :, lanes], now.at[:, pl.ds(zed, 4), t, core]),
+            (coef_hbm.at[:, :, :, lanes], coef.at[pl.ds(0, 2), pl.ds(own_c, 8), t, core]),
+            (zcoef_hbm.at[:, :, :, lanes], coef.at[:, pl.ds(zed_c, 2), t, core]),
+        ]
         if stretched:
-            fetch(stretch_hbm.at[:, :, lanes], coef.at[2, pl.ds(own_c, 8), t, core])
-    fetch(side_hbm.at[pl.ds(0, 3)], now.at[:, pl.ds(own, 8), tiles, core])
-    fetch(side_hbm.at[pl.ds(3, n_coef)], coef.at[:, pl.ds(own_c, 8), tiles, core])
-    fetch(zside_hbm.at[pl.ds(0, 3)], now.at[:, pl.ds(zed, 4), tiles, core])
-    fetch(zside_hbm.at[pl.ds(3, n_coef)], coef.at[:, pl.ds(8 - 8 * g, 4), tiles, core])
-    for copy in copies:
+            pairs.append((stretch_hbm.at[:, :, lanes], coef.at[2, pl.ds(own_c, 8), t, core]))
+        return [pltpu.make_async_copy(src, dst, sem.at[t, i]) for i, (src, dst) in enumerate(pairs)]
+
+    def side_fetches():
+        pairs = [
+            (side_hbm.at[pl.ds(0, 3)], now.at[:, pl.ds(own, 8), tiles, core]),
+            (zside_hbm.at[pl.ds(0, 3)], now.at[:, pl.ds(zed, 4), tiles, core]),
+            (side_hbm.at[pl.ds(3, n_coef)], coef.at[:, pl.ds(own_c, 8), tiles, core]),
+            (zside_hbm.at[pl.ds(3, n_coef)], coef.at[:, pl.ds(8 - 8 * g, 4), tiles, core]),
+        ]
+        return [pltpu.make_async_copy(src, dst, sem.at[tiles, i]) for i, (src, dst) in enumerate(pairs)]
+
+    prev_copy = pltpu.make_async_copy(prev_hbm, prev_ref, sem.at[tiles, 4])
+    for copy in side_fetches() + [copy for t in range(tiles) for copy in fetches(t)] + [prev_copy]:
         copy.start()
     for field in (now, acc):
         for z in (0, 1, 14, 15):
@@ -80,10 +86,11 @@
         ee[z] = jnp.zeros((ext, LANES), jnp.float32)
     near = near_base(g)
     n_now, width = 6 * (tiles + 1), tiles + 1
+    n_blocks = n_now + n_coef * width
     last = lax.axis_size("gx") - 1
     for ref, keep, at_now, at_coef in ((low_ref, gx > 0, 4, 6), (up_ref, gx < last, rows + 8, rows + 8)):
         zref = zlow_ref if ref is low_ref else zup_ref
-        groups = ((ref, block0, near), (ref, block0 + block_z, 4 - near), (zref, block0, 8 - 12 * g + 4 * g))
+        groups = ((ref, 0, near), (ref, n_blocks, 4 - near), (zref, 0, 8 - 8 * g))
         for source, base, layer in groups:
             first = layer if source is zref else layer + 4 * g
             for t in range(width):
@@ -96,7 +103,7 @@
                     v = jnp.where(keep, source[base + n_now + c * width + t], 0.0)
                     for h in range(4):
                         coef[c, first + h, t, pl.ds(at_coef, 2), :] = v[2 * h : 2 * h + 2]
-    for copy in copies:
+    for copy in side_fetches() + fetches(0):
         copy.wait()
 
     low_half = lax.broadcasted_iota(jnp.int32, (ext, LANES), 1) < 64
@@ -164,6 +171,11 @@
         lax.fori_loop(0, n, lambda i, carry: (f(i), carry)[1], 0)
 
     def first_pass(t):
+        @pl.when(t < tiles - 1)
+        def _():
+            for copy in fetches(t + 1):
+                copy.wait()
+
         loop(12 // C1, lambda i: y_stage(now, t, C1 * i, C1))
         loop(12, lambda z: mid_stage(now, t, z))
 
@@ -183,9 +195,16 @@
             total = 2.0 * now[c, z + 2, t, at, :] - previous(c) + DT2 * acc[c, z + 2, t, at, :] + DT4 * value
             store(c, total)
 
+    prev_copy.wait()
+    stores = []
     for t in range(tiles + 1):
-        loop(10 // C2, lambda i: y_stage(acc, t, C2 * i + 2 * g, C2))
-        loop(10, lambda i: mid_stage(acc, t, i + 2 * g))
+        if t < tiles:
+            loop(10 // C2, lambda i: y_stage(acc, t, C2 * i + 2 * g, C2))
+            loop(10, lambda i: mid_stage(acc, t, i + 2 * g))
+        else:
+            from_k = 4 if edge_k else 0
+            y_stage(acc, t, from_k + 4 * g, 4)
+            loop(4, lambda i: mid_stage(acc, t, from_k + i + 4 * g))
         if t < tiles:
             lanes = pl.ds(t * LANES, LANES)
 
@@ -200,6 +219,8 @@
                     finish(t, z, r, lambda c: prev_ref[c, k, at, lanes], store)
 
             loop(8, layer)
+            stores.append(pltpu.make_async_copy(step_ref.at[:, :, :, lanes], step_hbm.at[:, :, :, lanes], out_sem.at[t]))
+            stores[-1].start()
         else:
 
             def layer(i):
@@ -215,7 +236,23 @@
             loop(2, layer)
 
 
-def wave(now, coef, stretch, znow, zcoef, side, zside, low, up, zlow, zup, prev, prev4, edge_k, block0, block_z):
+    for t in range(tiles + 1):
+        lanes = pl.ds(t * LANES, LANES)
+        side = t == tiles
+        stiff = stiff4_ref[...] if side else stiff_ref[:, lanes]
+        for c in range(3):
+            ghost = ghost4_ref[c] if side else ghost_ref[c, :, lanes]
+            first, second = [edge_ref[c, i] if side else step_ref[c, edge_k + i, :, lanes] for i in range(2)]
+            plane_ref[c, :, lanes] = first + second
+            plane_ref[3 + c, :, lanes] = stiff * (ghost - first) if stretched else first + ghost
+        plane_ref[6, :, lanes] = stiff
+    for copy in stores:
+        copy.wait()
+
+
+def wave(
+    now, coef, stretch, znow, zcoef, side, zside, low, up, zlow, zup, prev, prev4, ghost, ghost4, stiff, stiff4, edge_k
+):
     rows, cols = prev.shape[2:]
     tiles = cols // LANES
     ext = rows + 16
@@ -225,14 +262,17 @@
     f32 = jnp.float32
     units = 3 * (10 * (ext - 8) // 8 * (tiles + 1) + rows * tiles)
     return pl.pallas_call(
-        functools.partial(wave_kernel, rows, tiles, stretched, edge_k, block0, block_z),
+        functools.partial(wave_kernel, rows, tiles, stretched, edge_k),
         out_shape=(
             jax.ShapeDtypeStruct((3, 8, rows, cols), f32),
-            jax.ShapeDtypeStruct((3, 2, rows, LANES), f32),
+            jax.ShapeDtypeStruct((7, rows, cols + LANES), f32),
         ),
-        in_specs=[hbm] * 7 + [vmem] * 7,
-        out_specs=(vmem, vmem),
+        in_specs=[hbm] * 7 + [vmem] * 4 + [hbm] + [vmem] * 6,
+        out_specs=(hbm, vmem),
         scratch_shapes=[
+            pltpu.VMEM((3, 8, rows, cols), f32),
+            pltpu.VMEM((3, 8, rows, cols), f32),
+            pltpu.VMEM((3, 2, rows, LANES), f32),
             pltpu.VMEM((3, 16, tiles + 1, ext, LANES), f32),
             pltpu.VMEM((3, 16, tiles + 1, ext, LANES), f32),
             pltpu.VMEM((zcoef.shape[0], 12, tiles + 1, ext, LANES), f32),
@@ -241,11 +281,15 @@
             pltpu.VMEM((12, ext, LANES), f32),
             pltpu.VMEM((16, ext, LANES), f32),
             pltpu.VMEM((max(C1, C2) * 6 * ext, 256), jnp.bfloat16),
-            pltpu.SemaphoreType.DMA((5 * tiles + 4,)),
+            pltpu.SemaphoreType.DMA((tiles + 1, 5)),
+            pltpu.SemaphoreType.DMA((tiles,)),
         ],
-        compiler_params=pltpu.CompilerParams(vmem_limit_bytes=56 * 2**20),
+        compiler_params=pltpu.CompilerParams(vmem_limit_bytes=58 * 2**20),
         cost_estimate=pl.CostEstimate(flops=units * 100000, bytes_accessed=10 * 2**20, transcendentals=0),
-    )(now, coef, stretch, znow, zcoef, side, zside, low, up, zlow, zup, prev, prev4, jnp.asarray(derivative_matrix(), jnp.bfloat16))
+    )(
+        now, coef, stretch, znow, zcoef, side, zside, low, up, zlow, zup, prev, prev4, ghost, ghost4, stiff, stiff4,
+        jnp.asarray(derivative_matrix(), jnp.bfloat16),
+    )
 
 
 def slots(widths):
@@ -350,7 +394,7 @@
     n = len(scales)
     for i, scale in enumerate(scales):
         mu, lam, rho = refs[3 * i : 3 * i + 3]
-        out = refs[3 * n + i]
+        out = refs[3 * n + 1 + i]
 
         def layer(z, carry, mu=mu, lam=lam, rho=rho, out=out, scale=scale):
             inverse = 1.0 / (scale * rho[z])
@@ -359,22 +403,27 @@
             return carry
 
         lax.fori_loop(0, 8, layer, 0)
-
-
-def coefficients(fine, coarse):
+    stretch, stiff, flex = refs[3 * n], refs[-2], refs[-1]
+    stiff[...] = refs[0][7] * stretch[0]
+    flex[...] = 2.0 / refs[3][0]
+
+
+def coefficients(fine, coarse, stretch):
     vmem = pl.BlockSpec(memory_space=pltpu.VMEM)
-    outs = tuple(jax.ShapeDtypeStruct((2,) + a[0].shape, jnp.float32) for a in (fine, coarse))
+    shapes = [(2,) + a[0].shape for a in (fine, coarse)] + [a[0].shape[1:] for a in (fine, coarse)]
     return pl.pallas_call(
-        functools.partial(coefficient_kernel, (12.0, 48.0)), out_shape=outs, in_specs=[vmem] * 6, out_specs=(vmem, vmem),
+        functools.partial(coefficient_kernel, (12.0, 48.0)),
+        out_shape=tuple(jax.ShapeDtypeStruct(a, jnp.float32) for a in shapes),
+        in_specs=[vmem] * 7, out_specs=(vmem,) * 4,
         compiler_params=pltpu.CompilerParams(vmem_limit_bytes=56 * 2**20),
         cost_estimate=pl.CostEstimate(flops=10**7, bytes_accessed=7 * 2**20, transcendentals=0),
-    )(*fine, *coarse)
+    )(*fine, *coarse, stretch)
 
 
 def unpack_kernel(*refs):
     from_up, from_low = refs[:2]
     fine_edges, coarse_edges = refs[2:8], refs[8:12]
-    fine_out, coarse_out, (low_ref, up_ref) = refs[12:16], refs[16:20], refs[20:]
+    fine_out, coarse_out, fine_msgs, coarse_msgs = refs[12:16], refs[16:20], refs[20:22], refs[22:]
     g = lax.axis_index("grid")
     gy = lax.axis_index("gy")
     keep_low, keep_up = gy > 0, gy < lax.axis_size("gy") - 1
@@ -400,12 +449,14 @@
             both = pltpu.roll(both, LANES - first, 1) if first else both
             valid = ((lane < hi) & keep_up) | ((lane >= LANES - lo) & keep_low)
             store(jnp.where(valid, both, 0.0))
-    base, far_base = 0, X_NEAR
-    for rows, width, n_coef, outs, edges in ((64, 5, 3, fine_out, fine_edges), (32, 3, 2, coarse_out, coarse_edges)):
+    for rows, width, n_coef, outs, edges, msgs in (
+        (64, 5, 3, fine_out, fine_edges, fine_msgs), (32, 3, 2, coarse_out, coarse_edges, coarse_msgs)
+    ):
         side_ref = outs[0]
+        half_blocks = (6 + n_coef) * width
         first_rows, last_rows = edges[0::2], edges[1::2]
-        for msg, edge, is_last in ((low_ref, first_rows, False), (up_ref, last_rows, True)):
-            for start, layer0 in ((base, near), (far_base, 4 - near)):
+        for msg, edge, is_last in ((msgs[0], first_rows, False), (msgs[1], last_rows, True)):
+            for start, layer0 in ((0, near), (half_blocks, 4 - near)):
                 for t in range(width):
                     lanes = pl.ds(t * LANES, LANES)
 
@@ -428,12 +479,10 @@
                     for c in range(n_coef):
                         parts = [rows_of(1, c, layer0 + h, 2) for h in range(4)]
                         msg[start + (6 + c) * width + t] = jnp.concatenate(parts, axis=0)
-        base += (6 + n_coef) * width
-        far_base += (6 + n_coef) * width
 
 
 X_FINE = 9 * 5
-X_NEAR = 9 * 5 + 8 * 3
+X_COARSE = 8 * 3
 
 
 def unpack(from_up, from_low, fine, coarse):
@@ -451,7 +500,7 @@
     shapes = []
     for rows, n_coef in ((64, 3), (32, 2)):
         shapes += [(3 + n_coef, 8, rows, LANES), (3, 2, rows, LANES), (3, rows, LANES), (rows, LANES)]
-    shapes += [(2 * X_NEAR, 8, LANES)] * 2
+    shapes += [(2 * X_FINE, 8, LANES)] * 2 + [(2 * X_COARSE, 8, LANES)] * 2
     return pl.pallas_call(
         unpack_kernel, grid=(1,),
         out_shape=tuple(jax.ShapeDtypeStruct(s, jnp.float32) for s in shapes),
@@ -513,84 +562,157 @@
     return out
 
 
+def times(rows, w_ref):
+    n = rows.shape[0]
+    high = rows.astype(jnp.bfloat16)
+    low = (rows - high.astype(jnp.float32)).astype(jnp.bfloat16)
+    out = jnp.dot(jnp.concatenate([high, low], axis=0), w_ref[...], preferred_element_type=jnp.float32)
+    return out[:n] + out[n:]
+
+
+def interface_kernel(*refs):
+    fine, coarse, (py_ref, ry_ref) = refs[0:6], refs[6:12], refs[12:14]
+    (out_fine, out_coarse, fine_plane, coarse_plane, tall, short, sem) = refs[16:]
+    g = lax.axis_index("grid")
+    gx = lax.axis_index("gx")
+    lower = g == 1
+    keep_low, keep_up = gx > 0, gx < lax.axis_size("gx") - 1
+    fine_rows, coarse_rows = tall.shape[1] - 16, short.shape[1]
+    half = fine_rows // 2
+
+    def grown(parts, i, own):
+        core, low, up = [jnp.where(own, parts[k][i], parts[3 + k][i]) for k in range(3)]
+        return jnp.concatenate([jnp.where(keep_low, low, 0.0), core, jnp.where(keep_up, up, 0.0)], axis=0)
+
+    def prolong(planes):
+        whole = []
+        for plane in planes:
+            parts = []
+            for t in range(plane.shape[1] // LANES):
+                short[t] = plane[:, t * LANES : (t + 1) * LANES]
+                at = lambda i: short[t, pl.ds(i, half), :]
+                tall[t, pl.ds(0, half, stride=2), :] = at(4)
+                tall[t, pl.ds(1, half, stride=2), :] = (9.0 * (at(4) + at(5)) - (at(3) + at(6))) * 0.0625
+                parts.append(tall[t, pl.ds(0, fine_rows), :])
+            whole.append(jnp.concatenate(parts, axis=1))
+        out = times(jnp.concatenate(whole, axis=0), py_ref)
+        return [out[c * fine_rows : (c + 1) * fine_rows] for c in range(3)]
+
+    def restrict(planes):
+        whole = []
+        for plane in planes:
+            parts = []
+            for t in range(plane.shape[1] // LANES):
+                tall[t, pl.ds(8, fine_rows), :] = plane[:, t * LANES : (t + 1) * LANES]
+                at = lambda i: tall[t, pl.ds(i, half, stride=2), :]
+                parts.append(0.25 * (at(7) + at(9)) + 0.5 * at(8))
+            whole.append(jnp.concatenate(parts, axis=1))
+        out = times(jnp.concatenate(whole, axis=0), ry_ref)
+        gap = jnp.zeros((4, out.shape[1]), jnp.float32)
+        return [jnp.concatenate([gap, out[c * half : (c + 1) * half], gap], axis=0) for c in range(3)]
+
+    tall[...] = jnp.zeros(tall.shape, jnp.float32)
+    own_coarse = jnp.logical_not(lower)
+    s, f = grown(fine, 6, lower), grown(coarse, 6, own_coarse)
+    u, w = [[grown(fine, 3 * k + c, lower) for c in range(3)] for k in range(2)]
+    p, q = [[grown(coarse, 3 * k + c, own_coarse) for c in range(3)] for k in range(2)]
+    r = restrict(w)
+    start = [jnp.where(lower, q[c], p[c] - r[c] * f) for c in range(3)]
+    v = prolong(start)
+    r = restrict([s * (v[c] - u[c]) for c in range(3)])
+    end = [p[c] - r[c] * f for c in range(3)]
+    v = prolong(end)
+    for c in range(3):
+        coarse_plane[c] = end[c][8:-8, : coarse_plane.shape[2]]
+        fine_plane[c] = v[c][8:-8, : fine_plane.shape[2]]
+
+    @pl.when(lower)
+    def _():
+        copy = pltpu.make_async_copy(fine_plane, out_fine.at[:, 7], sem)
+        copy.start()
+        copy.wait()
+
+    @pl.when(g == 0)
+    def _():
+        copy = pltpu.make_async_copy(coarse_plane, out_coarse.at[:, 0], sem)
+        copy.start()
+        copy.wait()
+
+
+def interface(fine, coarse, fine_step, coarse_step):
+    fine_rows, fine_cols = fine[0].shape[1] + 16, fine[0].shape[2]
+    coarse_rows, coarse_cols = coarse[0].shape[1] + 16, coarse[0].shape[2]
+    cyclic = lambda n: lambda i: i if i < n - LANES // 2 else i - n
+    cols = (coarse_cols, cyclic(coarse_cols), fine_cols, cyclic(fine_cols))
+    maps = (prolong_matrix(*cols).T, restrict_matrix(*cols).T)
+    vmem = pl.BlockSpec(memory_space=pltpu.VMEM)
+    hbm = pl.BlockSpec(memory_space=pl.ANY)
+    f32 = jnp.float32
+    return pl.pallas_call(
+        interface_kernel,
+        out_shape=tuple(jax.ShapeDtypeStruct(a.shape, f32) for a in (fine_step, coarse_step)),
+        in_specs=[vmem] * 14 + [hbm] * 2,
+        out_specs=(hbm, hbm),
+        input_output_aliases={14: 0, 15: 1},
+        scratch_shapes=[
+            pltpu.VMEM((3, fine_rows - 16, fine_cols - LANES), f32),
+            pltpu.VMEM((3, coarse_rows - 16, coarse_cols - LANES), f32),
+            pltpu.VMEM((fine_cols // LANES, fine_rows + 16, LANES), f32),
+            pltpu.VMEM((coarse_cols // LANES, coarse_rows, LANES), f32),
+            pltpu.SemaphoreType.DMA,
+        ],
+        compiler_params=pltpu.CompilerParams(vmem_limit_bytes=56 * 2**20),
+    )(*fine, *coarse, *[jnp.asarray(m, jnp.bfloat16) for m in maps], fine_step, coarse_step)
+
+
 def body(
     fine_now, fine_prev, fine_mu, fine_lam, fine_rho, fine_stretch,
     coarse_now, coarse_prev, coarse_mu, coarse_lam, coarse_rho, fine_ghost, coarse_ghost,
 ):
     g = lax.axis_index("grid")
-    upper = g == 0
-    wide = lambda a, b: jnp.concatenate([a, b], axis=-1)
-    stiff = fine_mu[7] * fine_stretch[7]
-    flex = 2.0 / coarse_mu[0]
     low, up = pack(
         (fine_now, fine_mu, fine_lam, fine_rho, fine_stretch, fine_prev, fine_ghost),
         (coarse_now, coarse_mu, coarse_lam, coarse_rho, coarse_prev, coarse_ghost),
     )
+    fine_now_z, coarse_now_z, low, up = lax.optimization_barrier((fine_now, coarse_now, low, up))
     from_up, from_low = ring(low, "gy", -1), ring(up, "gy", 1)
-    fine_coef, coarse_coef = coefficients((fine_mu, fine_lam, fine_rho), (coarse_mu, coarse_lam, coarse_rho))
+    fine_coef, coarse_coef, stiff, flex = coefficients(
+        (fine_mu, fine_lam, fine_rho), (coarse_mu, coarse_lam, coarse_rho), fine_stretch[7:]
+    )
     cut = lambda a, start, size: lax.dynamic_slice_in_dim(a, start, size, axis=1)
     near = near_base(g)
     near_c = 6 * (1 - g)
-    fine_z = swap(cut(fine_now, near, 4)), swap(cut(jnp.concatenate([fine_coef, fine_stretch[None]]), near_c, 2))
-    coarse_z = swap(cut(coarse_now, near, 4)), swap(cut(coarse_coef, near_c, 2))
-    (fine_side, fine_p4, fine_g4, fine_s4, coarse_side, coarse_p4, coarse_g4, coarse_s4, low, up) = unpack(
+    fine_z = swap(cut(fine_now_z, near, 4)), swap(cut(jnp.concatenate([fine_coef, fine_stretch[None]]), near_c, 2))
+    coarse_z = swap(cut(coarse_now_z, near, 4)), swap(cut(coarse_coef, near_c, 2))
+    (fine_side, fine_p4, fine_g4, fine_s4, coarse_side, coarse_p4, coarse_g4, coarse_s4,
+     fine_low, fine_up, coarse_low, coarse_up) = unpack(
         from_up, from_low, (fine_now, fine_coef, fine_stretch), (coarse_now, coarse_coef)
     )
-    from_up, from_low = ring(low, "gx", -1), ring(up, "gx", 1)
-    fine_zside, coarse_zside = swap(cut(fine_side, near, 4)), swap(cut(coarse_side, near, 4))
-    z_up, z_low = swap(from_up[:X_NEAR]), swap(from_low[:X_NEAR])
-    msgs = (from_low, from_up, z_low, z_up)
-    coarse_step, coarse_edge = wave(
-        coarse_now, coarse_coef, coarse_coef[0], *coarse_z, coarse_side, coarse_zside, *msgs, coarse_prev, coarse_p4,
-        0, X_FINE, X_NEAR,
+
+    def x_rings(low, up):
+        return ring(up, "gx", 1), ring(low, "gx", -1)
+
+    def x_halos(from_low, from_up):
+        n = from_low.shape[0] // 2
+        return from_low, from_up, swap(from_low[:n]), swap(from_up[:n])
+
+    def plane_halos(planes):
+        from_low, from_up = ring(planes[:, -8:], "gx", 1), ring(planes[:, :8], "gx", -1)
+        return planes, from_low, from_up, swap(planes), swap(from_low), swap(from_up)
+
+    coarse_x, fine_x = x_rings(coarse_low, coarse_up), x_rings(fine_low, fine_up)
+    coarse_zside, fine_zside = swap(cut(coarse_side, near, 4)), swap(cut(fine_side, near, 4))
+    coarse_step, coarse_planes = wave(
+        coarse_now, coarse_coef, coarse_coef[0], *coarse_z, coarse_side, coarse_zside, *x_halos(*coarse_x),
+        coarse_prev, coarse_p4, coarse_ghost, coarse_g4, flex, coarse_s4, 0,
     )
-    fine_step, fine_edge = wave(
-        fine_now, fine_coef, fine_stretch, *fine_z, fine_side, fine_zside, *msgs, fine_prev, fine_p4, 6, 0, X_NEAR
+    coarse_step, coarse_planes, *fine_x = lax.optimization_barrier((coarse_step, coarse_planes, *fine_x))
+    coarse_planes = plane_halos(coarse_planes)
+    fine_step, fine_planes = wave(
+        fine_now, fine_coef, fine_stretch, *fine_z, fine_side, fine_zside, *x_halos(*fine_x),
+        fine_prev, fine_p4, fine_ghost, fine_g4, stiff, fine_s4, 6,
     )
-
-    plane_fine = wide(fine_step[:, 7], fine_edge[:, 1])
-    above_fine = wide(fine_step[:, 6], fine_edge[:, 0])
-    plane_coarse = wide(coarse_step[:, 0], coarse_edge[:, 0])
-    below_coarse = wide(coarse_step[:, 1], coarse_edge[:, 1])
-    stiff = wide(stiff, fine_s4)
-    flex = wide(flex, coarse_s4)
-    fine_planes = jnp.concatenate(
-        [plane_fine + above_fine, stiff * (wide(fine_ghost, fine_g4) - above_fine), stiff[None]]
-    )
-    coarse_planes = jnp.concatenate(
-        [plane_coarse + below_coarse, plane_coarse + wide(coarse_ghost, coarse_g4), flex[None]]
-    )
-    (fl, fu), (cl, cu) = neighbours([(fine_planes, 1, 5, 4), (coarse_planes, 1, 3, 4)], "gx")
-    pad = lambda a, n, side: jnp.pad(a, ((0, 0), (n, 0) if side else (0, n), (0, 0)))
-    fine_planes = jnp.concatenate([pad(fl, 3, 1), fine_planes, pad(fu, 4, 0)], axis=1)
-    coarse_planes = jnp.concatenate([pad(cl, 1, 1), coarse_planes, cu], axis=1)
-    fine_other, coarse_other = swap(fine_planes), swap(coarse_planes)
-    fine_planes = jnp.where(upper, fine_other, fine_planes)
-    coarse_planes = jnp.where(upper, coarse_planes, coarse_other)
-
-    fine_rows, fine_cols = fine_planes.shape[1:]
-    coarse_rows, coarse_cols = coarse_planes.shape[1:]
-    at_rows = (lambda i: i - 4, lambda i: i - 8)
-    cyclic = lambda n: lambda i: i if i < n - LANES // 2 else i - n
-    at_cols = (cyclic(coarse_cols), cyclic(fine_cols))
-    px = prolong_matrix(coarse_rows, at_rows[0], fine_rows, at_rows[1])
-    py = prolong_matrix(coarse_cols, at_cols[0], fine_cols, at_cols[1])
-    rx = restrict_matrix(coarse_rows, at_rows[0], fine_rows, at_rows[1])
-    ry = restrict_matrix(coarse_cols, at_cols[0], fine_cols, at_cols[1])
-    both = lambda mx, my, v: jnp.einsum(
-        "ax,nxb->nab", mx, jnp.einsum("nxy,by->nxb", v, my, precision=HIGHEST), precision=HIGHEST
-    )
-    u, w, s = fine_planes[:3], fine_planes[3:6], fine_planes[6]
-    p, q, f = coarse_planes[:3], coarse_planes[3:6], coarse_planes[6]
-    start = jnp.where(upper, p - both(rx, ry, w) * f, q)
-    end = p - both(rx, ry, s * (both(px, py, start) - u)) * f
-    fine_plane = both(px, py, end)[:, 8:-8, :512]
-    coarse_plane = end[:, 4:-4, :256]
-    fine_out = jnp.where(upper, fine_step[:, 7], fine_plane)
-    coarse_out = jnp.where(upper, coarse_plane, coarse_step[:, 0])
-    fine_next = jnp.concatenate([fine_step[:, :7], fine_out[:, None]], axis=1)
-    coarse_next = jnp.concatenate([coarse_out[:, None], coarse_step[:, 1:]], axis=1)
-    return fine_next, coarse_next
+    return interface(plane_halos(fine_planes), coarse_planes, fine_step, coarse_step)
 
 
 def solution(mesh):

time: 138 us -> 121 us (0.88)
  starting transfers between devices: 17.2 us -> 27 us
  other arithmetic: 11.3 us -> 2.01 us
  matrix products: 6.87 us -> 0 us
  local copies, waits for them, and re-layouts: 20.4 us -> 13.6 us
  waiting for transfers between devices: 16.8 us -> 13.1 us
    ppermute x6 -> x10, waiting for transfers between devices: 16.8 us -> 6.84 us  [ring(): return lax.ppermute(value, axis, [(i, (i + by) % n) for i in range(n)])]
    dot_general x8 -> x0, matrix products: 6.87 us -> none  [the longest x4 4.81 us: body(): jnp.einsum('nxy,by->nxb', v, my, precision=HIGHEST)]
    ppermute x10 -> x16, waiting for transfers between devices: 0.03 us -> 6.26 us  [swap(): return lax.ppermute(value, 'grid', [(0, 1), (1, 0)])]
    ppermute x10 -> x16, starting transfers between devices: 4.26 us -> 10.1 us  [swap(): return lax.ppermute(value, 'grid', [(0, 1), (1, 0)])]
    concatenate x7 -> x0, other arithmetic: 5.04 us -> none  [the longest x1 1.97 us: body(): fine_next = jnp.concatenate([fine_step[:, :7], fine_out[:, None]], axis=1)]
    pallas_call x0 -> x1, Pallas kernels: none -> 4.78 us  [interface(): pl.pallas_call(interface_kernel, out_shape=tuple((jax.ShapeDtypeStruct(a....]
    pallas_call x2, Pallas kernels: 50.6 us -> 46.5 us  [wave(): pl.pallas_call(functools.partial(wave_kernel, rows, tiles, stretched, edg...]
    ppermute x6 -> x10, starting transfers between devices: 12.9 us -> 16.9 us  [ring(): return lax.ppermute(value, axis, [(i, (i + by) % n) for i in range(n)])]
  transfers between devices with their start and end apart: 16 -> 26, of which waited for: 3 -> 9; matrix products, arithmetic and copies ran while one was open for 13% -> 8% of each run, Pallas kernels for 17% -> 19%
where the time goes in v1:
time: 121 us
  Pallas kernels  64.1 us (53%)
  starting transfers between devices  27 us (22%)
  local copies, waits for them, and re-layouts  13.6 us (11%)
  waiting for transfers between devices  13.1 us (11%)
  other arithmetic  2.01 us (2%)
    pallas_call x2, Pallas kernels, wave(): pl.pallas_call(functools.partial(wave_kernel, rows, tiles, stretched, edg...  46.5 us
    ppermute x10, starting transfers between devices, ring(): return lax.ppermute(value, axis, [(i, (i + by) % n) for i in range(n)])  16.9 us
    ppermute x16, starting transfers between devices, swap(): return lax.ppermute(value, 'grid', [(0, 1), (1, 0)])  10.1 us
    ppermute x10, waiting for transfers between devices, ring(): return lax.ppermute(value, axis, [(i, (i + by) % n) for i in range(n)])  6.84 us
    ppermute x16, waiting for transfers between devices, swap(): return lax.ppermute(value, 'grid', [(0, 1), (1, 0)])  6.26 us
    dynamic_slice x5, local copies, waits for them, and re-layouts, body(): lax.dynamic_slice_in_dim(a, start, size, axis=1)  5.24 us
    unnamed x62, local copies, waits for them, and re-layouts  5.05 us
    pallas_call x1, Pallas kernels, interface(): pl.pallas_call(interface_kernel, out_shape=tuple((jax.ShapeDtypeStruct(a....  4.78 us
  transfers between devices with their start and end apart: 26, of which 9 were waited for; matrix products, arithmetic and copies ran while one was open for 8% of the time, Pallas kernels for 19%

profile of v1, /device:TPU:1, one launch (start us, length us, event | category | flops | bytes accessed | tf_op | source)
XLA Modules:
  0.0 120.9 jit_solution(7022018243301794082)
XLA Ops:
  0.6 4.5 %shard_map.177 = (f32[44,8,128]{2,1,0:T(8,128)}, f32[44,8,128]{2,1,0:T(8,128)}) custom-call(f32[3,8,64,512]{3,2,1,0:T(8,128)} %refs_0_.7, f32[3,8,64,512]{3,2,1,0:T(8,128)} %refs_0_.7, f32[8,64,512]{2,1,0:T(8,128)} %refs_3_.4, f32[8,64,512]{2,1,0:T(8,128)} %refs_3_.4, f32[8,64,512]{2,1,0:T(8,128)} %refs_5_.3, f32[8,64,512]{2,1,0:T(8,128)} %refs_5_.3, ...), custom_call_target="tpu_custom_call" | custom-call | tf_op jit(solution)/shard_map/pallas_call | solution.py:387
  5.1 1.4 %constant_dynamic-slice_fusion.4 = f32[3,4,64,512]{3,2,1,0:T(8,128)} fusion(f32[3,8,64,512]{3,2,1,0:T(8,128)S(1)} %copy-done, s32[]{:T(128)S(6)} %select_n.4), kind=kLoop, calls=%fused_computation.8 | loop fusion | bytes 3145732 | tf_op jit(solution)/shard_map/dynamic_slice | solution.py:682
  6.5 1.4 %collective-permute-start = (f32[3,4,64,512]{3,2,1,0:T(8,128)}, f32[3,4,64,512]{3,2,1,0:T(8,128)S(1)}, u32[]{:S(2)}, u32[]{:S(2)}) collective-permute-start(f32[3,4,64,512]{3,2,1,0:T(8,128)} %constant_dynamic-slice_fusion.4), channel_id=1, source_target_pairs={{0,1},{1,0},{2,3},{3,2},{4,5},{5,4},{6,7},{7,6},{8,9},{9,8},{10,11... | collective-permute-start | bytes 4718600 | tf_op jit(solution)/shard_map/ppermute | solution.py:519
  7.9 5.9 %collective-permute-start.2 = (f32[44,8,128]{2,1,0:T(8,128)}, f32[44,8,128]{2,1,0:T(8,128)S(1)}, u32[]{:S(2)}, u32[]{:S(2)}) collective-permute-start(f32[44,8,128]{2,1,0:T(8,128)} %get-tuple-element.36), channel_id=1, source_target_pairs={{0,14},{2,0},{4,2},{6,4},{8,6},{10,8},{12,10},{14,12},{1,15},{3,1}... | collective-permute-start | bytes 540680 | tf_op jit(solution)/shard_map/ppermute | solution.py:515
  14.9 1.6 %slice.30.refs_6_ = f32[1,64,512]{2,1,0:T(8,128)} slice(f32[8,64,512]{2,1,0:T(8,128)} %refs_2_.7), slice={[7:8], [0:64], [0:512]} | slice | bytes 262144 | tf_op jit(solution)/shard_map/slice | solution.py:680
  16.4 4.1 %shard_map.176 = (f32[2,8,64,512]{3,2,1,0:T(8,128)}, f32[2,8,32,256]{3,2,1,0:T(8,128)}, f32[64,512]{1,0:T(8,128)}, f32[32,256]{1,0:T(8,128)}) custom-call(f32[8,64,512]{2,1,0:T(8,128)} %refs_3_.4, f32[8,64,512]{2,1,0:T(8,128)} %refs_5_.3, f32[8,64,512]{2,1,0:T(8,128)} %refs_7_.2, f32[8,32,256]{2,1,0:T(8,128)} %refs_17_.3, f32[8,32,256]{2,1,0:T(8,128)} %refs_19_.1, ...), custom_call_target="tpu_custom_call" | custom-call | flops 10000000 | bytes 7340032 | tf_op jit(solution)/shard_map/pallas_call | solution.py:414
  21.8 2.0 %fusion = f32[3,2,64,512]{3,2,1,0:T(8,128)} fusion(s32[]{:T(128)S(6)} %select_n.5, f32[2,8,64,512]{3,2,1,0:T(8,128)} %get-tuple-element.32.refs_4_.refs_5_.refs_1_, f32[1,8,64,512]{3,2,1,0:T(8,128)S(1)} %bitcast.3), kind=kLoop, calls=%fused_computation.2 | loop fusion | flops 196608 | bytes 3932164 | tf_op jit(solution)/shard_map/concatenate | solution.py:685
  25.1 4.3 %shard_map.178 = (f32[6,8,64,128]{3,2,1,0:T(8,128)}, f32[3,2,64,128]{3,2,1,0:T(8,128)}, f32[3,64,128]{2,1,0:T(8,128)}, f32[64,128]{1,0:T(8,128)}, f32[5,8,32,128...) custom-call(f32[44,8,128]{2,1,0:T(8,128)} %copy-done.18, ...), custom_call_target="tpu_custom_call" | custom-call | tf_op jit(solution)/shard_map/pallas_call | solution.py:504
  29.4 1.4 %collective-permute-start.8 = (f32[48,8,128]{2,1,0:T(8,128)}, f32[48,8,128]{2,1,0:T(8,128)S(1)}, u32[]{:S(2)}, u32[]{:S(2)}) collective-permute-start(f32[48,8,128]{2,1,0:T(8,128)} %get-tuple-element.42), channel_id=1, source_target_pairs={{0,16},{16,32},{32,48},{48,64},{64,80},{80,96},{96,112},{112,0},{1... | collective-permute-start | bytes 589832 | tf_op jit(solution)/shard_map/ppermute | solution.py:515
  30.8 2.3 %collective-permute-start.9 = (f32[48,8,128]{2,1,0:T(8,128)}, f32[48,8,128]{2,1,0:T(8,128)S(1)}, u32[]{:S(2)}, u32[]{:S(2)}) collective-permute-start(f32[48,8,128]{2,1,0:T(8,128)} %get-tuple-element.43), channel_id=1, source_target_pairs={{0,112},{16,0},{32,16},{48,32},{64,48},{80,64},{96,80},{112,96},{1... | collective-permute-start | bytes 589832 | tf_op jit(solution)/shard_map/ppermute | solution.py:515
  35.0 1.2 constant_dynamic-slice_fusion.3
  36.2 1.8 %collective-permute-done.8.refs_7_ = f32[48,8,128]{2,1,0:T(8,128)S(1)} collective-permute-done((f32[48,8,128]{2,1,0:T(8,128)}, f32[48,8,128]{2,1,0:T(8,128)S(1)}, u32[]{:S(2)}, u32[]{:S(2)}) %collective-permute-start.8) | collective-permute-done | bytes 196640 | tf_op jit(solution)/shard_map/ppermute | solution.py:515
  38.0 1.1 collective-permute-start.1
  39.7 2.5 %collective-permute-done.10.refs_9_ = f32[24,8,128]{2,1,0:T(8,128)S(1)} collective-permute-done((f32[24,8,128]{2,1,0:T(8,128)S(1)}, f32[24,8,128]{2,1,0:T(8,128)S(1)}, u32[]{:S(2)}, u32[]{:S(2)}) %collective-permute-start.10) | collective-permute-done | bytes 98336 | tf_op jit(solution)/shard_map/ppermute | solution.py:519
  44.4 3.6 %collective-permute-start.13 = (f32[90,8,128]{2,1,0:T(8,128)}, f32[90,8,128]{2,1,0:T(8,128)S(1)}, u32[]{:S(2)}, u32[]{:S(2)}) collective-permute-start(f32[90,8,128]{2,1,0:T(8,128)} %get-tuple-element.51), channel_id=1, source_target_pairs={{0,112},{16,0},{32,16},{48,32},{64,48},{80,64},{96,80},{112,96},{1... | collective-permute-start | bytes 1105928 | tf_op jit(solution)/shard_map/ppermute | solution.py:515
  48.7 14.1 %shard_map.179 = (f32[3,8,32,256]{3,2,1,0:T(8,128)}, f32[7,32,384]{2,1,0:T(8,128)}) custom-call(f32[3,8,32,256]{3,2,1,0:T(8,128)} %refs_0_.6, f32[2,8,32,256]{3,2,1,0:T(8,128)} %get-tuple-element.38.refs_10_.refs_11_.refs_1_, f32[8,32,256]{2,1,0:T(8,128)} %slice_bitcast_fusion.refs_2_, f32[3,4,32,256]{3,2,1,0:T(8,128)} %copy-done.13, ...), custom_call_target="tpu_custom_call" | custom-call | flops 64200000 | bytes 10485760 | tf_op jit(solution)/shard_map/pallas_call | solution.py:264
  62.8 1.0 collective-permute-start.14
  67.3 32.4 %shard_map.180 = (f32[3,8,64,512]{3,2,1,0:T(8,128)}, f32[7,64,640]{2,1,0:T(8,128)}) custom-call(f32[3,8,64,512]{3,2,1,0:T(8,128)} %refs_0_.7, f32[2,8,64,512]{3,2,1,0:T(8,128)} %get-tuple-element.32.refs_4_.refs_5_.refs_1_, f32[8,64,512]{2,1,0:T(8,128)} %refs_2_.7, f32[3,4,64,512]{3,2,1,0:T(8,128)} %copy-done.4, f32[3,2,64,512]{3,2,1,0:T(8,128)} %copy-done.8, ...), custom_call_target="tpu_custom_call" | custom-call | flops 211800000 | bytes 10485760 | tf_op jit(solution)/shard_map/pallas_call | solution.py:264
  100.4 1.0 fusion.1
  101.5 3.6 %collective-permute-start.17 = (f32[7,8,640]{2,1,0:T(8,128)S(1)}, f32[7,8,640]{2,1,0:T(8,128)S(1)}, u32[]{:S(2)}, u32[]{:S(2)}) collective-permute-start(f32[7,8,640]{2,1,0:T(8,128)S(1)} %get-tuple-element.62), channel_id=1, source_target_pairs={{0,112},{16,0},{32,16},{48,32},{64,48},{80,64},{96,80},{112,96},{1... | collective-permute-start | bytes 430088 | tf_op jit(solution)/shard_map/ppermute | solution.py:515
  105.1 1.4 %collective-permute-done.21.refs_7_ = f32[7,8,384]{2,1,0:T(8,128)S(1)} collective-permute-done((f32[7,8,384]{2,1,0:T(8,128)S(1)}, f32[7,8,384]{2,1,0:T(8,128)S(1)}, u32[]{:S(2)}, u32[]{:S(2)}) %collective-permute-start.21) | collective-permute-done | bytes 86048 | tf_op jit(solution)/shard_map/ppermute | solution.py:515
  106.5 3.6 %collective-permute-done.22.refs_8_ = f32[7,8,384]{2,1,0:T(8,128)S(1)} collective-permute-done((f32[7,8,384]{2,1,0:T(8,128)S(1)}, f32[7,8,384]{2,1,0:T(8,128)S(1)}, u32[]{:S(2)}, u32[]{:S(2)}) %collective-permute-start.22) | collective-permute-done | bytes 86048 | tf_op jit(solution)/shard_map/ppermute | solution.py:515
  110.1 2.4 %collective-permute-start.24 = (f32[7,8,384]{2,1,0:T(8,128)S(1)}, f32[7,8,384]{2,1,0:T(8,128)S(1)}, u32[]{:S(2)}, u32[]{:S(2)}) collective-permute-start(f32[7,8,384]{2,1,0:T(8,128)S(1)} %collective-permute-done.21.refs_7_), channel_id=1, source_target_pairs={{0,1},{1,0},{2,3},{3,2},{4,5},{5,4},{6,7},{7,6},{8,9},{9,8},{10,11... | collective-permute-start | bytes 258056 | tf_op jit(solution)/shard_map/ppermute | solution.py:519
  116.0 4.8 %shard_map.181 = (f32[3,8,64,512]{3,2,1,0:T(8,128)}, f32[3,8,32,256]{3,2,1,0:T(8,128)}) custom-call(f32[7,64,640]{2,1,0:T(8,128)} %get-tuple-element.58.refs_0_, f32[7,8,640]{2,1,0:T(8,128)} %copy-done.20, f32[7,8,640]{2,1,0:T(8,128)} %copy-done.21, f32[7,64,640]{2,1,0:T(8,128)} %copy-done.5, ...), custom_call_target="tpu_custom_call", output_to_operand_aliasing={{0}: (14, {}), {1}: (15, {})} | custom-call | tf_op jit(solution)/shard_map/pallas_call | solution.py:651
  (110 shorter events, 16.6 us)
Async XLA Ops:
  6.5 59.1 %collective-permute-start = (f32[3,4,64,512]{3,2,1,0:T(8,128)}, f32[3,4,64,512]{3,2,1,0:T(8,128)S(1)}, u32[]{:S(2)}, u32[]{:S(2)}) collective-permute-start(f32[3,4,64,512]{3,2,1,0:T(8,128)} %constant_dynamic-slice_fusion.4), channel_id=1, source_target_pairs={{0,1},{1,0},{2,3},{3,2},{4,5},{5,4},{6,7},{7,6},{8,9},{9,8},{10,11... | collective-permute-start | bytes 4718600 | tf_op jit(solution)/shard_map/ppermute | solution.py:519
  7.9 15.8 %collective-permute-start.2 = (f32[44,8,128]{2,1,0:T(8,128)}, f32[44,8,128]{2,1,0:T(8,128)S(1)}, u32[]{:S(2)}, u32[]{:S(2)}) collective-permute-start(f32[44,8,128]{2,1,0:T(8,128)} %get-tuple-element.36), channel_id=1, source_target_pairs={{0,14},{2,0},{4,2},{6,4},{8,6},{10,8},{12,10},{14,12},{1,15},{3,1}... | collective-permute-start | bytes 540680 | tf_op jit(solution)/shard_map/ppermute | solution.py:515
  13.8 10.0 %collective-permute-start.3 = (f32[44,8,128]{2,1,0:T(8,128)}, f32[44,8,128]{2,1,0:T(8,128)S(1)}, u32[]{:S(2)}, u32[]{:S(2)}) collective-permute-start(f32[44,8,128]{2,1,0:T(8,128)} %get-tuple-element.37), channel_id=1, source_target_pairs={{0,2},{2,4},{4,6},{6,8},{8,10},{10,12},{12,14},{14,0},{1,3},{3,5},... | collective-permute-start | bytes 540680 | tf_op jit(solution)/shard_map/ppermute | solution.py:515
  14.6 24.6 %collective-permute-start.5 = (f32[3,4,32,256]{3,2,1,0:T(8,128)}, f32[3,4,32,256]{3,2,1,0:T(8,128)S(1)}, u32[]{:S(2)}, u32[]{:S(2)}) collective-permute-start(f32[3,4,32,256]{3,2,1,0:T(8,128)} %constant_dynamic-slice_fusion.2), channel_id=1, source_target_pairs={{0,1},{1,0},{2,3},{3,2},{4,5},{5,4},{6,7},{7,6},{8,9},{9,8},{10,11... | collective-permute-start | bytes 1179656 | tf_op jit(solution)/shard_map/ppermute | solution.py:519
  21.4 12.6 %collective-permute-start.6 = (f32[2,2,32,256]{3,2,1,0:T(8,128)S(1)}, f32[2,2,32,256]{3,2,1,0:T(8,128)S(1)}, u32[]{:S(2)}, u32[]{:S(2)}) collective-permute-start(f32[2,2,32,256]{3,2,1,0:T(8,128)S(1)} %constant_dynamic-slice_fusion.1), channel_id=1, source_target_pairs={{0,1},{1,0},{2,3},{3,2},{4,5},{5,4},{6,7},{7,6},{8,9},{9,8},{10,11... | collective-permute-start | bytes 393224 | tf_op jit(solution)/shard_map/ppermute | solution.py:519
  29.4 8.6 %collective-permute-start.8 = (f32[48,8,128]{2,1,0:T(8,128)}, f32[48,8,128]{2,1,0:T(8,128)S(1)}, u32[]{:S(2)}, u32[]{:S(2)}) collective-permute-start(f32[48,8,128]{2,1,0:T(8,128)} %get-tuple-element.42), channel_id=1, source_target_pairs={{0,16},{16,32},{32,48},{48,64},{64,80},{80,96},{96,112},{112,0},{1... | collective-permute-start | bytes 589832 | tf_op jit(solution)/shard_map/ppermute | solution.py:515
  30.8 8.3 %collective-permute-start.9 = (f32[48,8,128]{2,1,0:T(8,128)}, f32[48,8,128]{2,1,0:T(8,128)S(1)}, u32[]{:S(2)}, u32[]{:S(2)}) collective-permute-start(f32[48,8,128]{2,1,0:T(8,128)} %get-tuple-element.43), channel_id=1, source_target_pairs={{0,112},{16,0},{32,16},{48,32},{64,48},{80,64},{96,80},{112,96},{1... | collective-permute-start | bytes 589832 | tf_op jit(solution)/shard_map/ppermute | solution.py:515
  34.1 9.6 %collective-permute-start.7 = (f32[5,4,32,128]{3,2,1,0:T(8,128)S(1)}, f32[5,4,32,128]{3,2,1,0:T(8,128)S(1)}, u32[]{:S(2)}, u32[]{:S(2)}) collective-permute-start(f32[5,4,32,128]{3,2,1,0:T(8,128)S(1)} %constant_dynamic-slice_fusion), channel_id=1, source_target_pairs={{0,1},{1,0},{2,3},{3,2},{4,5},{5,4},{6,7},{7,6},{8,9},{9,8},{10,11... | collective-permute-start | bytes 983048 | tf_op jit(solution)/shard_map/ppermute | solution.py:519
  38.0 27.5 %collective-permute-start.1 = (f32[3,2,64,512]{3,2,1,0:T(8,128)}, f32[3,2,64,512]{3,2,1,0:T(8,128)S(1)}, u32[]{:S(2)}, u32[]{:S(2)}) collective-permute-start(f32[3,2,64,512]{3,2,1,0:T(8,128)} %fusion), channel_id=1, source_target_pairs={{0,1},{1,0},{2,3},{3,2},{4,5},{5,4},{6,7},{7,6},{8,9},{9,8},{10,11... | collective-permute-start | bytes 2359304 | tf_op jit(solution)/shard_map/ppermute | solution.py:519
  39.1 26.4 %collective-permute-start.4 = (f32[6,4,64,128]{3,2,1,0:T(8,128)S(1)}, f32[6,4,64,128]{3,2,1,0:T(8,128)S(1)}, u32[]{:S(2)}, u32[]{:S(2)}) collective-permute-start(f32[6,4,64,128]{3,2,1,0:T(8,128)S(1)} %constant_dynamic-slice_fusion.3), channel_id=1, source_target_pairs={{0,1},{1,0},{2,3},{3,2},{4,5},{5,4},{6,7},{7,6},{8,9},{9,8},{10,11... | collective-permute-start | bytes 2359304 | tf_op jit(solution)/shard_map/ppermute | solution.py:519
  39.2 3.1 %collective-permute-start.10 = (f32[24,8,128]{2,1,0:T(8,128)S(1)}, f32[24,8,128]{2,1,0:T(8,128)S(1)}, u32[]{:S(2)}, u32[]{:S(2)}) collective-permute-start(f32[24,8,128]{2,1,0:T(8,128)S(1)} %slice.40), channel_id=1, source_target_pairs={{0,1},{1,0},{2,3},{3,2},{4,5},{5,4},{6,7},{7,6},{8,9},{9,8},{10,11... | collective-permute-start | bytes 294920 | tf_op jit(solution)/shard_map/ppermute | solution.py:519
  43.6 19.2 %collective-permute-start.12 = (f32[90,8,128]{2,1,0:T(8,128)}, f32[90,8,128]{2,1,0:T(8,128)S(1)}, u32[]{:S(2)}, u32[]{:S(2)}) collective-permute-start(f32[90,8,128]{2,1,0:T(8,128)} %get-tuple-element.50), channel_id=1, source_target_pairs={{0,16},{16,32},{32,48},{48,64},{64,80},{80,96},{96,112},{112,0},{1... | collective-permute-start | bytes 1105928 | tf_op jit(solution)/shard_map/ppermute | solution.py:515
  44.4 18.4 %collective-permute-start.13 = (f32[90,8,128]{2,1,0:T(8,128)}, f32[90,8,128]{2,1,0:T(8,128)S(1)}, u32[]{:S(2)}, u32[]{:S(2)}) collective-permute-start(f32[90,8,128]{2,1,0:T(8,128)} %get-tuple-element.51), channel_id=1, source_target_pairs={{0,112},{16,0},{32,16},{48,32},{64,48},{80,64},{96,80},{112,96},{1... | collective-permute-start | bytes 1105928 | tf_op jit(solution)/shard_map/ppermute | solution.py:515
  62.8 2.1 %collective-permute-start.14 = (f32[45,8,128]{2,1,0:T(8,128)S(1)}, f32[45,8,128]{2,1,0:T(8,128)S(1)}, u32[]{:S(2)}, u32[]{:S(2)}) collective-permute-start(f32[45,8,128]{2,1,0:T(8,128)S(1)} %slice.34), channel_id=1, source_target_pairs={{0,1},{1,0},{2,3},{3,2},{4,5},{5,4},{6,7},{7,6},{8,9},{9,8},{10,11... | collective-permute-start | bytes 552968 | tf_op jit(solution)/shard_map/ppermute | solution.py:519
  63.8 1.7 %collective-permute-start.15 = (f32[45,8,128]{2,1,0:T(8,128)S(1)}, f32[45,8,128]{2,1,0:T(8,128)S(1)}, u32[]{:S(2)}, u32[]{:S(2)}) collective-permute-start(f32[45,8,128]{2,1,0:T(8,128)S(1)} %slice.35), channel_id=1, source_target_pairs={{0,1},{1,0},{2,3},{3,2},{4,5},{5,4},{6,7},{7,6},{8,9},{9,8},{10,11... | collective-permute-start | bytes 552968 | tf_op jit(solution)/shard_map/ppermute | solution.py:519
  99.7 15.0 %collective-permute-start.18 = (f32[7,64,640]{2,1,0:T(8,128)}, f32[7,64,640]{2,1,0:T(8,128)S(1)}, u32[]{:S(2)}, u32[]{:S(2)}) collective-permute-start(f32[7,64,640]{2,1,0:T(8,128)} %get-tuple-element.58.refs_0_), channel_id=1, source_target_pairs={{0,1},{1,0},{2,3},{3,2},{4,5},{5,4},{6,7},{7,6},{8,9},{9,8},{10,11... | collective-permute-start | bytes 3440648 | tf_op jit(solution)/shard_map/ppermute | solution.py:519
  100.0 14.8 %collective-permute-start.23 = (f32[7,32,384]{2,1,0:T(8,128)S(1)}, f32[7,32,384]{2,1,0:T(8,128)S(1)}, u32[]{:S(2)}, u32[]{:S(2)}) collective-permute-start(f32[7,32,384]{2,1,0:T(8,128)S(1)} %copy-done.10), channel_id=1, source_target_pairs={{0,1},{1,0},{2,3},{3,2},{4,5},{5,4},{6,7},{7,6},{8,9},{9,8},{10,11... | collective-permute-start | bytes 1032200 | tf_op jit(solution)/shard_map/ppermute | solution.py:519
  100.3 6.2 %collective-permute-start.21 = (f32[7,8,384]{2,1,0:T(8,128)S(1)}, f32[7,8,384]{2,1,0:T(8,128)S(1)}, u32[]{:S(2)}, u32[]{:S(2)}) collective-permute-start(f32[7,8,384]{2,1,0:T(8,128)S(1)} %get-tuple-element.65), channel_id=1, source_target_pairs={{0,16},{16,32},{32,48},{48,64},{64,80},{80,96},{96,112},{112,0},{1... | collective-permute-start | bytes 258056 | tf_op jit(solution)/shard_map/ppermute | solution.py:515
  101.4 11.1 %collective-permute-start.16 = (f32[7,8,640]{2,1,0:T(8,128)S(1)}, f32[7,8,640]{2,1,0:T(8,128)S(1)}, u32[]{:S(2)}, u32[]{:S(2)}) collective-permute-start(f32[7,8,640]{2,1,0:T(8,128)S(1)} %get-tuple-element.63), channel_id=1, source_target_pairs={{0,16},{16,32},{32,48},{48,64},{64,80},{80,96},{96,112},{112,0},{1... | collective-permute-start | bytes 430088 | tf_op jit(solution)/shard_map/ppermute | solution.py:515
  101.5 11.1 %collective-permute-start.17 = (f32[7,8,640]{2,1,0:T(8,128)S(1)}, f32[7,8,640]{2,1,0:T(8,128)S(1)}, u32[]{:S(2)}, u32[]{:S(2)}) collective-permute-start(f32[7,8,640]{2,1,0:T(8,128)S(1)} %get-tuple-element.62), channel_id=1, source_target_pairs={{0,112},{16,0},{32,16},{48,32},{64,48},{80,64},{96,80},{112,96},{1... | collective-permute-start | bytes 430088 | tf_op jit(solution)/shard_map/ppermute | solution.py:515
  106.5 3.6 %collective-permute-start.22 = (f32[7,8,384]{2,1,0:T(8,128)S(1)}, f32[7,8,384]{2,1,0:T(8,128)S(1)}, u32[]{:S(2)}, u32[]{:S(2)}) collective-permute-start(f32[7,8,384]{2,1,0:T(8,128)S(1)} %get-tuple-element.64), channel_id=1, source_target_pairs={{0,112},{16,0},{32,16},{48,32},{64,48},{80,64},{96,80},{112,96},{1... | collective-permute-start | bytes 258056 | tf_op jit(solution)/shard_map/ppermute | solution.py:515
  110.1 3.3 %collective-permute-start.24 = (f32[7,8,384]{2,1,0:T(8,128)S(1)}, f32[7,8,384]{2,1,0:T(8,128)S(1)}, u32[]{:S(2)}, u32[]{:S(2)}) collective-permute-start(f32[7,8,384]{2,1,0:T(8,128)S(1)} %collective-permute-done.21.refs_7_), channel_id=1, source_target_pairs={{0,1},{1,0},{2,3},{3,2},{4,5},{5,4},{6,7},{7,6},{8,9},{9,8},{10,11... | collective-permute-start | bytes 258056 | tf_op jit(solution)/shard_map/ppermute | solution.py:519
  112.5 2.2 %collective-permute-start.19 = (f32[7,8,640]{2,1,0:T(8,128)S(1)}, f32[7,8,640]{2,1,0:T(8,128)S(1)}, u32[]{:S(2)}, u32[]{:S(2)}) collective-permute-start(f32[7,8,640]{2,1,0:T(8,128)S(1)} %collective-permute-done.16.refs_1_), channel_id=1, source_target_pairs={{0,1},{1,0},{2,3},{3,2},{4,5},{5,4},{6,7},{7,6},{8,9},{9,8},{10,11... | collective-permute-start | bytes 430088 | tf_op jit(solution)/shard_map/ppermute | solution.py:519
  112.6 2.1 %collective-permute-start.20 = (f32[7,8,640]{2,1,0:T(8,128)S(1)}, f32[7,8,640]{2,1,0:T(8,128)S(1)}, u32[]{:S(2)}, u32[]{:S(2)}) collective-permute-start(f32[7,8,640]{2,1,0:T(8,128)S(1)} %collective-permute-done.17.refs_2_), channel_id=1, source_target_pairs={{0,1},{1,0},{2,3},{3,2},{4,5},{5,4},{6,7},{7,6},{8,9},{9,8},{10,11... | collective-permute-start | bytes 430088 | tf_op jit(solution)/shard_map/ppermute | solution.py:519
  (33 other events, 159.0 us)

commit v2 on v1

--- a/solution.py
+++ b/solution.py
@@ -420,16 +420,15 @@
     )(*fine, *coarse, stretch)
 
 
-def unpack_kernel(*refs):
+def unpack_kernel(rows, halo, n_coef, block0, *refs):
     from_up, from_low = refs[:2]
-    fine_edges, coarse_edges = refs[2:8], refs[8:12]
-    fine_out, coarse_out, fine_msgs, coarse_msgs = refs[12:16], refs[16:20], refs[20:22], refs[22:]
+    edges, outs, msgs = refs[2:-6], refs[-6:-2], refs[-2:]
     g = lax.axis_index("grid")
     gy = lax.axis_index("gy")
     keep_low, keep_up = gy > 0, gy < lax.axis_size("gy") - 1
     near = near_base(g)
-    block0 = 0
-    for rows, halo, n_coef, outs in ((64, FINE_HALO, 3, fine_out), (32, COARSE_HALO, 2, coarse_out)):
+    width = 5 if n_coef == 3 else 3
+    if True:
         halos, places, n_tiles = items_of(halo, n_coef)
         lane = lax.broadcasted_iota(jnp.int32, (rows, LANES), 1)
         side_ref, prev_ref, ghost_ref, stiff_ref = outs
@@ -449,9 +448,7 @@
             both = pltpu.roll(both, LANES - first, 1) if first else both
             valid = ((lane < hi) & keep_up) | ((lane >= LANES - lo) & keep_low)
             store(jnp.where(valid, both, 0.0))
-    for rows, width, n_coef, outs, edges, msgs in (
-        (64, 5, 3, fine_out, fine_edges, fine_msgs), (32, 3, 2, coarse_out, coarse_edges, coarse_msgs)
-    ):
+    if True:
         side_ref = outs[0]
         half_blocks = (6 + n_coef) * width
         first_rows, last_rows = edges[0::2], edges[1::2]
@@ -481,32 +478,28 @@
                         msg[start + (6 + c) * width + t] = jnp.concatenate(parts, axis=0)
 
 
-X_FINE = 9 * 5
-X_COARSE = 8 * 3
-
-
-def unpack(from_up, from_low, fine, coarse):
-    vmem = pl.BlockSpec(memory_space=pltpu.VMEM)
+def unpack(from_up, from_low, arrays, halo, block0):
+    rows, cols = arrays[0].shape[2:]
+    n_coef = len(arrays)
     specs, operands = [], []
-    whole = pl.BlockSpec((Y_BLOCKS, 8, LANES), lambda i: (0, 0, 0))
-    for arrays in (fine, coarse):
-        for a in arrays:
-            block = list(a.shape)
-            block[-2] = 8
-            for tile in (0, a.shape[-2] // 8 - 1):
-                where = tuple([0] * (a.ndim - 2) + [tile, 0])
-                specs.append(pl.BlockSpec(tuple(block), lambda i, where=where: where))
-                operands.append(a)
-    shapes = []
-    for rows, n_coef in ((64, 3), (32, 2)):
-        shapes += [(3 + n_coef, 8, rows, LANES), (3, 2, rows, LANES), (3, rows, LANES), (rows, LANES)]
-    shapes += [(2 * X_FINE, 8, LANES)] * 2 + [(2 * X_COARSE, 8, LANES)] * 2
+    blocks = from_up.shape[0]
+    whole = pl.BlockSpec((blocks, 8, LANES), lambda i: (0, 0, 0))
+    for a in arrays:
+        block = list(a.shape)
+        block[-2] = 8
+        for tile in (0, rows // 8 - 1):
+            where = tuple([0] * (a.ndim - 2) + [tile, 0])
+            specs.append(pl.BlockSpec(tuple(block), lambda i, where=where: where))
+            operands.append(a)
+    shapes = [(3 + n_coef, 8, rows, LANES), (3, 2, rows, LANES), (3, rows, LANES), (rows, LANES)]
+    shapes += [(2 * (6 + n_coef) * (cols // LANES + 1), 8, LANES)] * 2
     return pl.pallas_call(
-        unpack_kernel, grid=(1,),
+        functools.partial(unpack_kernel, rows, halo, n_coef, block0), grid=(1,),
         out_shape=tuple(jax.ShapeDtypeStruct(s, jnp.float32) for s in shapes),
         in_specs=[whole, whole] + specs,
         out_specs=tuple(pl.BlockSpec(s, lambda i, n=len(s): (0,) * n) for s in shapes),
         compiler_params=pltpu.CompilerParams(vmem_limit_bytes=56 * 2**20),
+        cost_estimate=pl.CostEstimate(flops=rows * 10**5, bytes_accessed=rows * 2**16, transcendentals=0),
     )(from_up, from_low, *operands)
 
 
@@ -684,9 +677,11 @@
     near_c = 6 * (1 - g)
     fine_z = swap(cut(fine_now_z, near, 4)), swap(cut(jnp.concatenate([fine_coef, fine_stretch[None]]), near_c, 2))
     coarse_z = swap(cut(coarse_now_z, near, 4)), swap(cut(coarse_coef, near_c, 2))
-    (fine_side, fine_p4, fine_g4, fine_s4, coarse_side, coarse_p4, coarse_g4, coarse_s4,
-     fine_low, fine_up, coarse_low, coarse_up) = unpack(
-        from_up, from_low, (fine_now, fine_coef, fine_stretch), (coarse_now, coarse_coef)
+    coarse_side, coarse_p4, coarse_g4, coarse_s4, coarse_low, coarse_up = unpack(
+        from_up, from_low, (coarse_now, coarse_coef), COARSE_HALO, 8 * items_of(FINE_HALO, 3)[2]
+    )
+    fine_side, fine_p4, fine_g4, fine_s4, fine_low, fine_up = unpack(
+        from_up, from_low, (fine_now, fine_coef, fine_stretch), FINE_HALO, 0
     )
 
     def x_rings(low, up):

time: 121 us -> 120 us (level)
  Pallas kernels: 64.1 us -> 65.9 us
  waiting for transfers between devices: 13.1 us -> 11.5 us
    ppermute x10, waiting for transfers between devices: 6.84 us -> 4.98 us  [ring(): return lax.ppermute(value, axis, [(i, (i + by) % n) for i in range(n)])]
    pallas_call x1 -> x2, Pallas kernels: 4.27 us -> 6.11 us  [unpack(): pl.pallas_call(functools.partial(unpack_kernel, rows, halo, n_coef, block...]
    unnamed x62 -> x64, local copies, waits for them, and re-layouts: 5.05 us -> 5.08 us
  transfers between devices with their start and end apart: 26 -> 26, of which waited for: 9 -> 8; matrix products, arithmetic and copies ran while one was open for 8% -> 7% of each run, Pallas kernels for 19% -> 20%
where the time goes in v2:
time: 120 us; the launch traced here: 119 us
  Pallas kernels  65.9 us (55%)
  starting transfers between devices  25.9 us (22%)
  local copies, waits for them, and re-layouts  12.7 us (11%)
  waiting for transfers between devices  11.5 us (10%)
  other arithmetic  2.01 us (2%)
    pallas_call x2, Pallas kernels, wave(): pl.pallas_call(functools.partial(wave_kernel, rows, tiles, stretched, edg...  46.5 us
    ppermute x10, starting transfers between devices, ring(): return lax.ppermute(value, axis, [(i, (i + by) % n) for i in range(n)])  16.8 us
    ppermute x16, starting transfers between devices, swap(): return lax.ppermute(value, 'grid', [(0, 1), (1, 0)])  9.12 us
    ppermute x16, waiting for transfers between devices, swap(): return lax.ppermute(value, 'grid', [(0, 1), (1, 0)])  6.48 us
    pallas_call x2, Pallas kernels, unpack(): pl.pallas_call(functools.partial(unpack_kernel, rows, halo, n_coef, block...  6.11 us
    unnamed x64, local copies, waits for them, and re-layouts  5.08 us
    ppermute x10, waiting for transfers between devices, ring(): return lax.ppermute(value, axis, [(i, (i + by) % n) for i in range(n)])  4.98 us
    pallas_call x1, Pallas kernels, interface(): pl.pallas_call(interface_kernel, out_shape=tuple((jax.ShapeDtypeStruct(a....  4.79 us
  transfers between devices with their start and end apart: 26, of which 8 were waited for; matrix products, arithmetic and copies ran while one was open for 7% of the time, Pallas kernels for 20%

profile of v2, /device:TPU:1, one launch (start us, length us, event | category | flops | bytes accessed | tf_op | source)
XLA Modules:
  0.0 119.2 jit_solution(12377262181099928334)
XLA Ops:
  0.6 4.5 %shard_map.177 = (f32[44,8,128]{2,1,0:T(8,128)}, f32[44,8,128]{2,1,0:T(8,128)}) custom-call(f32[3,8,64,512]{3,2,1,0:T(8,128)} %refs_0_.7, f32[3,8,64,512]{3,2,1,0:T(8,128)} %refs_0_.7, f32[8,64,512]{2,1,0:T(8,128)} %refs_3_.5, f32[8,64,512]{2,1,0:T(8,128)} %refs_3_.5, f32[8,64,512]{2,1,0:T(8,128)} %refs_5_.3, f32[8,64,512]{2,1,0:T(8,128)} %refs_5_.3, ...), custom_call_target="tpu_custom_call" | custom-call | tf_op jit(solution)/shard_map/pallas_call | solution.py:387
  5.1 1.4 %constant_dynamic-slice_fusion.4 = f32[3,4,64,512]{3,2,1,0:T(8,128)} fusion(f32[3,8,64,512]{3,2,1,0:T(8,128)S(1)} %copy-done, s32[]{:T(128)S(6)} %select_n.4), kind=kLoop, calls=%fused_computation.8 | loop fusion | bytes 3145732 | tf_op jit(solution)/shard_map/dynamic_slice | solution.py:675
  6.5 1.4 %collective-permute-start = (f32[3,4,64,512]{3,2,1,0:T(8,128)}, f32[3,4,64,512]{3,2,1,0:T(8,128)S(1)}, u32[]{:S(2)}, u32[]{:S(2)}) collective-permute-start(f32[3,4,64,512]{3,2,1,0:T(8,128)} %constant_dynamic-slice_fusion.4), channel_id=1, source_target_pairs={{0,1},{1,0},{2,3},{3,2},{4,5},{5,4},{6,7},{7,6},{8,9},{9,8},{10,11... | collective-permute-start | bytes 4718600 | tf_op jit(solution)/shard_map/ppermute | solution.py:512
  7.9 5.9 %collective-permute-start.2 = (f32[44,8,128]{2,1,0:T(8,128)}, f32[44,8,128]{2,1,0:T(8,128)S(1)}, u32[]{:S(2)}, u32[]{:S(2)}) collective-permute-start(f32[44,8,128]{2,1,0:T(8,128)} %get-tuple-element.36), channel_id=1, source_target_pairs={{0,14},{2,0},{4,2},{6,4},{8,6},{10,8},{12,10},{14,12},{1,15},{3,1}... | collective-permute-start | bytes 540680 | tf_op jit(solution)/shard_map/ppermute | solution.py:508
  14.9 1.6 %slice.30.refs_6_ = f32[1,64,512]{2,1,0:T(8,128)} slice(f32[8,64,512]{2,1,0:T(8,128)} %refs_2_.9), slice={[7:8], [0:64], [0:512]} | slice | bytes 262144 | tf_op jit(solution)/shard_map/slice | solution.py:673
  16.4 4.1 %shard_map.176 = (f32[2,8,64,512]{3,2,1,0:T(8,128)}, f32[2,8,32,256]{3,2,1,0:T(8,128)}, f32[64,512]{1,0:T(8,128)}, f32[32,256]{1,0:T(8,128)}) custom-call(f32[8,64,512]{2,1,0:T(8,128)} %refs_3_.5, f32[8,64,512]{2,1,0:T(8,128)} %refs_5_.3, f32[8,64,512]{2,1,0:T(8,128)} %refs_7_.2, f32[8,32,256]{2,1,0:T(8,128)} %refs_17_.3, f32[8,32,256]{2,1,0:T(8,128)} %refs_19_.1, ...), custom_call_target="tpu_custom_call" | custom-call | flops 10000000 | bytes 7340032 | tf_op jit(solution)/shard_map/pallas_call | solution.py:414
  21.8 2.0 %fusion = f32[3,2,64,512]{3,2,1,0:T(8,128)} fusion(s32[]{:T(128)S(6)} %select_n.5, f32[2,8,64,512]{3,2,1,0:T(8,128)} %get-tuple-element.32.refs_4_.refs_5_.refs_1_, f32[1,8,64,512]{3,2,1,0:T(8,128)S(1)} %bitcast.3), kind=kLoop, calls=%fused_computation.2 | loop fusion | flops 196608 | bytes 3932164 | tf_op jit(solution)/shard_map/concatenate | solution.py:678
  25.1 2.6 %shard_map.179 = (f32[5,8,32,128]{3,2,1,0:T(8,128)}, f32[3,2,32,128]{3,2,1,0:T(8,128)}, f32[3,32,128]{2,1,0:T(8,128)}, f32[32,128]{1,0:T(8,128)}, f32[48,8,128]{2,1,0:T(8,128)}, /*index=5*/f32[48,8,128]{2,1,0:T(8,128)}) custom-call(f32[44,8,128]{2,1,0:T(8,128)} %copy-done.12, f32[44,8,128]{2,1,0:T(8,128)} %copy-done.13, f32[3,8,32,256]{3,2,1,0:T(8,128)} %refs_0_.6, ...), custom_call_target="tpu_custom_call" | custom-call | flops 3200000 | bytes 2097152 | tf_op jit(solution)/shard_map/pallas_call | solution.py:496
  27.7 1.3 %collective-permute-start.8 = (f32[48,8,128]{2,1,0:T(8,128)}, f32[48,8,128]{2,1,0:T(8,128)S(1)}, u32[]{:S(2)}, u32[]{:S(2)}) collective-permute-start(f32[48,8,128]{2,1,0:T(8,128)} %get-tuple-element.42), channel_id=1, source_target_pairs={{0,16},{16,32},{32,48},{48,64},{64,80},{80,96},{96,112},{112,0},{1... | collective-permute-start | bytes 589832 | tf_op jit(solution)/shard_map/ppermute | solution.py:508
  29.0 2.3 %collective-permute-start.9 = (f32[48,8,128]{2,1,0:T(8,128)}, f32[48,8,128]{2,1,0:T(8,128)S(1)}, u32[]{:S(2)}, u32[]{:S(2)}) collective-permute-start(f32[48,8,128]{2,1,0:T(8,128)} %get-tuple-element.43), channel_id=1, source_target_pairs={{0,112},{16,0},{32,16},{48,32},{64,48},{80,64},{96,80},{112,96},{1... | collective-permute-start | bytes 589832 | tf_op jit(solution)/shard_map/ppermute | solution.py:508
  31.3 3.5 %shard_map.178 = (f32[6,8,64,128]{3,2,1,0:T(8,128)}, f32[3,2,64,128]{3,2,1,0:T(8,128)}, f32[3,64,128]{2,1,0:T(8,128)}, f32[64,128]{1,0:T(8,128)}, f32[90,8,128]{2,1,0:T(8,128)}, /*index=5*/f32[90,8,128]{2,1,0:T(8,128)}) custom-call(f32[44,8,128]{2,1,0:T(8,128)} %copy-done.12, f32[44,8,128]{2,1,0:T(8,128)} %copy-done.13, f32[3,8,64,512]{3,2,1,0:T(8,128)} %refs_0_.7, ...), custom_call_target="tpu_custom_call" | custom-call | flops 6400000 | bytes 4194304 | tf_op jit(solution)/shard_map/pallas_call | solution.py:496
  35.8 1.2 constant_dynamic-slice_fusion.3
  38.0 2.7 %collective-permute-done.10.refs_9_ = f32[24,8,128]{2,1,0:T(8,128)S(1)} collective-permute-done((f32[24,8,128]{2,1,0:T(8,128)S(1)}, f32[24,8,128]{2,1,0:T(8,128)S(1)}, u32[]{:S(2)}, u32[]{:S(2)}) %collective-permute-start.10) | collective-permute-done | bytes 98336 | tf_op jit(solution)/shard_map/ppermute | solution.py:512
  40.9 1.0 collective-permute-done.11.refs_10_
  42.7 3.6 %collective-permute-start.13 = (f32[90,8,128]{2,1,0:T(8,128)}, f32[90,8,128]{2,1,0:T(8,128)S(1)}, u32[]{:S(2)}, u32[]{:S(2)}) collective-permute-start(f32[90,8,128]{2,1,0:T(8,128)} %get-tuple-element.51), channel_id=1, source_target_pairs={{0,112},{16,0},{32,16},{48,32},{64,48},{80,64},{96,80},{112,96},{1... | collective-permute-start | bytes 1105928 | tf_op jit(solution)/shard_map/ppermute | solution.py:508
  47.1 14.1 %shard_map.180 = (f32[3,8,32,256]{3,2,1,0:T(8,128)}, f32[7,32,384]{2,1,0:T(8,128)}) custom-call(f32[3,8,32,256]{3,2,1,0:T(8,128)} %refs_0_.6, f32[2,8,32,256]{3,2,1,0:T(8,128)} %get-tuple-element.39.refs_4_.refs_5_.refs_1_, f32[8,32,256]{2,1,0:T(8,128)} %slice_bitcast_fusion.refs_2_, f32[3,4,32,256]{3,2,1,0:T(8,128)} %copy-done.16, ...), custom_call_target="tpu_custom_call" | custom-call | flops 64200000 | bytes 10485760 | tf_op jit(solution)/shard_map/pallas_call | solution.py:264
  65.6 32.4 %shard_map.181 = (f32[3,8,64,512]{3,2,1,0:T(8,128)}, f32[7,64,640]{2,1,0:T(8,128)}) custom-call(f32[3,8,64,512]{3,2,1,0:T(8,128)} %refs_0_.7, f32[2,8,64,512]{3,2,1,0:T(8,128)} %get-tuple-element.32.refs_4_.refs_5_.refs_1_, f32[8,64,512]{2,1,0:T(8,128)} %refs_2_.9, f32[3,4,64,512]{3,2,1,0:T(8,128)} %copy-done.4, f32[3,2,64,512]{3,2,1,0:T(8,128)} %copy-done.9, ...), custom_call_target="tpu_custom_call" | custom-call | flops 211800000 | bytes 10485760 | tf_op jit(solution)/shard_map/pallas_call | solution.py:264
  98.7 1.0 fusion.1
  99.8 3.6 %collective-permute-start.17 = (f32[7,8,640]{2,1,0:T(8,128)S(1)}, f32[7,8,640]{2,1,0:T(8,128)S(1)}, u32[]{:S(2)}, u32[]{:S(2)}) collective-permute-start(f32[7,8,640]{2,1,0:T(8,128)S(1)} %get-tuple-element.62), channel_id=1, source_target_pairs={{0,112},{16,0},{32,16},{48,32},{64,48},{80,64},{96,80},{112,96},{1... | collective-permute-start | bytes 430088 | tf_op jit(solution)/shard_map/ppermute | solution.py:508
  103.4 1.4 %collective-permute-done.21.refs_7_ = f32[7,8,384]{2,1,0:T(8,128)S(1)} collective-permute-done((f32[7,8,384]{2,1,0:T(8,128)S(1)}, f32[7,8,384]{2,1,0:T(8,128)S(1)}, u32[]{:S(2)}, u32[]{:S(2)}) %collective-permute-start.21) | collective-permute-done | bytes 86048 | tf_op jit(solution)/shard_map/ppermute | solution.py:508
  104.8 3.6 %collective-permute-done.22.refs_8_ = f32[7,8,384]{2,1,0:T(8,128)S(1)} collective-permute-done((f32[7,8,384]{2,1,0:T(8,128)S(1)}, f32[7,8,384]{2,1,0:T(8,128)S(1)}, u32[]{:S(2)}, u32[]{:S(2)}) %collective-permute-start.22) | collective-permute-done | bytes 86048 | tf_op jit(solution)/shard_map/ppermute | solution.py:508
  108.4 2.4 %collective-permute-start.24 = (f32[7,8,384]{2,1,0:T(8,128)S(1)}, f32[7,8,384]{2,1,0:T(8,128)S(1)}, u32[]{:S(2)}, u32[]{:S(2)}) collective-permute-start(f32[7,8,384]{2,1,0:T(8,128)S(1)} %collective-permute-done.21.refs_7_), channel_id=1, source_target_pairs={{0,1},{1,0},{2,3},{3,2},{4,5},{5,4},{6,7},{7,6},{8,9},{9,8},{10,11... | collective-permute-start | bytes 258056 | tf_op jit(solution)/shard_map/ppermute | solution.py:512
  112.1 0.9 collective-permute-done.25.refs_11_
  114.3 4.8 %shard_map.182 = (f32[3,8,64,512]{3,2,1,0:T(8,128)}, f32[3,8,32,256]{3,2,1,0:T(8,128)}) custom-call(f32[7,64,640]{2,1,0:T(8,128)} %get-tuple-element.58.refs_0_, f32[7,8,640]{2,1,0:T(8,128)} %copy-done.21, f32[7,8,640]{2,1,0:T(8,128)} %copy-done.22, f32[7,64,640]{2,1,0:T(8,128)} %copy-done.6, ...), custom_call_target="tpu_custom_call", output_to_operand_aliasing={{0}: (14, {}), {1}: (15, {})} | custom-call | tf_op jit(solution)/shard_map/pallas_call | solution.py:644
  (113 shorter events, 15.0 us)
Async XLA Ops:
  6.5 57.3 %collective-permute-start = (f32[3,4,64,512]{3,2,1,0:T(8,128)}, f32[3,4,64,512]{3,2,1,0:T(8,128)S(1)}, u32[]{:S(2)}, u32[]{:S(2)}) collective-permute-start(f32[3,4,64,512]{3,2,1,0:T(8,128)} %constant_dynamic-slice_fusion.4), channel_id=1, source_target_pairs={{0,1},{1,0},{2,3},{3,2},{4,5},{5,4},{6,7},{7,6},{8,9},{9,8},{10,11... | collective-permute-start | bytes 4718600 | tf_op jit(solution)/shard_map/ppermute | solution.py:512
  7.9 15.8 %collective-permute-start.2 = (f32[44,8,128]{2,1,0:T(8,128)}, f32[44,8,128]{2,1,0:T(8,128)S(1)}, u32[]{:S(2)}, u32[]{:S(2)}) collective-permute-start(f32[44,8,128]{2,1,0:T(8,128)} %get-tuple-element.36), channel_id=1, source_target_pairs={{0,14},{2,0},{4,2},{6,4},{8,6},{10,8},{12,10},{14,12},{1,15},{3,1}... | collective-permute-start | bytes 540680 | tf_op jit(solution)/shard_map/ppermute | solution.py:508
  13.8 10.0 %collective-permute-start.3 = (f32[44,8,128]{2,1,0:T(8,128)}, f32[44,8,128]{2,1,0:T(8,128)S(1)}, u32[]{:S(2)}, u32[]{:S(2)}) collective-permute-start(f32[44,8,128]{2,1,0:T(8,128)} %get-tuple-element.37), channel_id=1, source_target_pairs={{0,2},{2,4},{4,6},{6,8},{8,10},{10,12},{12,14},{14,0},{1,3},{3,5},... | collective-permute-start | bytes 540680 | tf_op jit(solution)/shard_map/ppermute | solution.py:508
  14.6 23.0 %collective-permute-start.5 = (f32[3,4,32,256]{3,2,1,0:T(8,128)}, f32[3,4,32,256]{3,2,1,0:T(8,128)S(1)}, u32[]{:S(2)}, u32[]{:S(2)}) collective-permute-start(f32[3,4,32,256]{3,2,1,0:T(8,128)} %constant_dynamic-slice_fusion.2), channel_id=1, source_target_pairs={{0,1},{1,0},{2,3},{3,2},{4,5},{5,4},{6,7},{7,6},{8,9},{9,8},{10,11... | collective-permute-start | bytes 1179656 | tf_op jit(solution)/shard_map/ppermute | solution.py:512
  21.4 13.4 %collective-permute-start.6 = (f32[2,2,32,256]{3,2,1,0:T(8,128)S(1)}, f32[2,2,32,256]{3,2,1,0:T(8,128)S(1)}, u32[]{:S(2)}, u32[]{:S(2)}) collective-permute-start(f32[2,2,32,256]{3,2,1,0:T(8,128)S(1)} %constant_dynamic-slice_fusion.1), channel_id=1, source_target_pairs={{0,1},{1,0},{2,3},{3,2},{4,5},{5,4},{6,7},{7,6},{8,9},{9,8},{10,11... | collective-permute-start | bytes 393224 | tf_op jit(solution)/shard_map/ppermute | solution.py:512
  27.7 9.3 %collective-permute-start.8 = (f32[48,8,128]{2,1,0:T(8,128)}, f32[48,8,128]{2,1,0:T(8,128)S(1)}, u32[]{:S(2)}, u32[]{:S(2)}) collective-permute-start(f32[48,8,128]{2,1,0:T(8,128)} %get-tuple-element.42), channel_id=1, source_target_pairs={{0,16},{16,32},{32,48},{48,64},{64,80},{80,96},{96,112},{112,0},{1... | collective-permute-start | bytes 589832 | tf_op jit(solution)/shard_map/ppermute | solution.py:508
  29.0 8.3 %collective-permute-start.9 = (f32[48,8,128]{2,1,0:T(8,128)}, f32[48,8,128]{2,1,0:T(8,128)S(1)}, u32[]{:S(2)}, u32[]{:S(2)}) collective-permute-start(f32[48,8,128]{2,1,0:T(8,128)} %get-tuple-element.43), channel_id=1, source_target_pairs={{0,112},{16,0},{32,16},{48,32},{64,48},{80,64},{96,80},{112,96},{1... | collective-permute-start | bytes 589832 | tf_op jit(solution)/shard_map/ppermute | solution.py:508
  34.9 7.1 %collective-permute-start.7 = (f32[5,4,32,128]{3,2,1,0:T(8,128)S(1)}, f32[5,4,32,128]{3,2,1,0:T(8,128)S(1)}, u32[]{:S(2)}, u32[]{:S(2)}) collective-permute-start(f32[5,4,32,128]{3,2,1,0:T(8,128)S(1)} %constant_dynamic-slice_fusion), channel_id=1, source_target_pairs={{0,1},{1,0},{2,3},{3,2},{4,5},{5,4},{6,7},{7,6},{8,9},{9,8},{10,11... | collective-permute-start | bytes 983048 | tf_op jit(solution)/shard_map/ppermute | solution.py:512
  37.0 26.8 %collective-permute-start.1 = (f32[3,2,64,512]{3,2,1,0:T(8,128)}, f32[3,2,64,512]{3,2,1,0:T(8,128)S(1)}, u32[]{:S(2)}, u32[]{:S(2)}) collective-permute-start(f32[3,2,64,512]{3,2,1,0:T(8,128)} %fusion), channel_id=1, source_target_pairs={{0,1},{1,0},{2,3},{3,2},{4,5},{5,4},{6,7},{7,6},{8,9},{9,8},{10,11... | collective-permute-start | bytes 2359304 | tf_op jit(solution)/shard_map/ppermute | solution.py:512
  37.4 26.5 %collective-permute-start.4 = (f32[6,4,64,128]{3,2,1,0:T(8,128)S(1)}, f32[6,4,64,128]{3,2,1,0:T(8,128)S(1)}, u32[]{:S(2)}, u32[]{:S(2)}) collective-permute-start(f32[6,4,64,128]{3,2,1,0:T(8,128)S(1)} %constant_dynamic-slice_fusion.3), channel_id=1, source_target_pairs={{0,1},{1,0},{2,3},{3,2},{4,5},{5,4},{6,7},{7,6},{8,9},{9,8},{10,11... | collective-permute-start | bytes 2359304 | tf_op jit(solution)/shard_map/ppermute | solution.py:512
  37.6 3.0 %collective-permute-start.10 = (f32[24,8,128]{2,1,0:T(8,128)S(1)}, f32[24,8,128]{2,1,0:T(8,128)S(1)}, u32[]{:S(2)}, u32[]{:S(2)}) collective-permute-start(f32[24,8,128]{2,1,0:T(8,128)S(1)} %slice.40), channel_id=1, source_target_pairs={{0,1},{1,0},{2,3},{3,2},{4,5},{5,4},{6,7},{7,6},{8,9},{9,8},{10,11... | collective-permute-start | bytes 294920 | tf_op jit(solution)/shard_map/ppermute | solution.py:512
  42.0 19.2 %collective-permute-start.12 = (f32[90,8,128]{2,1,0:T(8,128)}, f32[90,8,128]{2,1,0:T(8,128)S(1)}, u32[]{:S(2)}, u32[]{:S(2)}) collective-permute-start(f32[90,8,128]{2,1,0:T(8,128)} %get-tuple-element.50), channel_id=1, source_target_pairs={{0,16},{16,32},{32,48},{48,64},{64,80},{80,96},{96,112},{112,0},{1... | collective-permute-start | bytes 1105928 | tf_op jit(solution)/shard_map/ppermute | solution.py:508
  42.7 18.5 %collective-permute-start.13 = (f32[90,8,128]{2,1,0:T(8,128)}, f32[90,8,128]{2,1,0:T(8,128)S(1)}, u32[]{:S(2)}, u32[]{:S(2)}) collective-permute-start(f32[90,8,128]{2,1,0:T(8,128)} %get-tuple-element.51), channel_id=1, source_target_pairs={{0,112},{16,0},{32,16},{48,32},{64,48},{80,64},{96,80},{112,96},{1... | collective-permute-start | bytes 1105928 | tf_op jit(solution)/shard_map/ppermute | solution.py:508
  61.2 1.9 %collective-permute-start.14 = (f32[45,8,128]{2,1,0:T(8,128)S(1)}, f32[45,8,128]{2,1,0:T(8,128)S(1)}, u32[]{:S(2)}, u32[]{:S(2)}) collective-permute-start(f32[45,8,128]{2,1,0:T(8,128)S(1)} %slice.34), channel_id=1, source_target_pairs={{0,1},{1,0},{2,3},{3,2},{4,5},{5,4},{6,7},{7,6},{8,9},{9,8},{10,11... | collective-permute-start | bytes 552968 | tf_op jit(solution)/shard_map/ppermute | solution.py:512
  62.1 1.7 %collective-permute-start.15 = (f32[45,8,128]{2,1,0:T(8,128)S(1)}, f32[45,8,128]{2,1,0:T(8,128)S(1)}, u32[]{:S(2)}, u32[]{:S(2)}) collective-permute-start(f32[45,8,128]{2,1,0:T(8,128)S(1)} %slice.35), channel_id=1, source_target_pairs={{0,1},{1,0},{2,3},{3,2},{4,5},{5,4},{6,7},{7,6},{8,9},{9,8},{10,11... | collective-permute-start | bytes 552968 | tf_op jit(solution)/shard_map/ppermute | solution.py:512
  98.0 15.1 %collective-permute-start.18 = (f32[7,64,640]{2,1,0:T(8,128)}, f32[7,64,640]{2,1,0:T(8,128)S(1)}, u32[]{:S(2)}, u32[]{:S(2)}) collective-permute-start(f32[7,64,640]{2,1,0:T(8,128)} %get-tuple-element.58.refs_0_), channel_id=1, source_target_pairs={{0,1},{1,0},{2,3},{3,2},{4,5},{5,4},{6,7},{7,6},{8,9},{9,8},{10,11... | collective-permute-start | bytes 3440648 | tf_op jit(solution)/shard_map/ppermute | solution.py:512
  98.2 14.8 %collective-permute-start.23 = (f32[7,32,384]{2,1,0:T(8,128)S(1)}, f32[7,32,384]{2,1,0:T(8,128)S(1)}, u32[]{:S(2)}, u32[]{:S(2)}) collective-permute-start(f32[7,32,384]{2,1,0:T(8,128)S(1)} %copy-done.11), channel_id=1, source_target_pairs={{0,1},{1,0},{2,3},{3,2},{4,5},{5,4},{6,7},{7,6},{8,9},{9,8},{10,11... | collective-permute-start | bytes 1032200 | tf_op jit(solution)/shard_map/ppermute | solution.py:512
  98.6 6.2 %collective-permute-start.21 = (f32[7,8,384]{2,1,0:T(8,128)S(1)}, f32[7,8,384]{2,1,0:T(8,128)S(1)}, u32[]{:S(2)}, u32[]{:S(2)}) collective-permute-start(f32[7,8,384]{2,1,0:T(8,128)S(1)} %get-tuple-element.65), channel_id=1, source_target_pairs={{0,16},{16,32},{32,48},{48,64},{64,80},{80,96},{96,112},{112,0},{1... | collective-permute-start | bytes 258056 | tf_op jit(solution)/shard_map/ppermute | solution.py:508
  99.7 11.1 %collective-permute-start.16 = (f32[7,8,640]{2,1,0:T(8,128)S(1)}, f32[7,8,640]{2,1,0:T(8,128)S(1)}, u32[]{:S(2)}, u32[]{:S(2)}) collective-permute-start(f32[7,8,640]{2,1,0:T(8,128)S(1)} %get-tuple-element.63), channel_id=1, source_target_pairs={{0,16},{16,32},{32,48},{48,64},{64,80},{80,96},{96,112},{112,0},{1... | collective-permute-start | bytes 430088 | tf_op jit(solution)/shard_map/ppermute | solution.py:508
  99.8 11.1 %collective-permute-start.17 = (f32[7,8,640]{2,1,0:T(8,128)S(1)}, f32[7,8,640]{2,1,0:T(8,128)S(1)}, u32[]{:S(2)}, u32[]{:S(2)}) collective-permute-start(f32[7,8,640]{2,1,0:T(8,128)S(1)} %get-tuple-element.62), channel_id=1, source_target_pairs={{0,112},{16,0},{32,16},{48,32},{64,48},{80,64},{96,80},{112,96},{1... | collective-permute-start | bytes 430088 | tf_op jit(solution)/shard_map/ppermute | solution.py:508
  104.8 3.6 %collective-permute-start.22 = (f32[7,8,384]{2,1,0:T(8,128)S(1)}, f32[7,8,384]{2,1,0:T(8,128)S(1)}, u32[]{:S(2)}, u32[]{:S(2)}) collective-permute-start(f32[7,8,384]{2,1,0:T(8,128)S(1)} %get-tuple-element.64), channel_id=1, source_target_pairs={{0,112},{16,0},{32,16},{48,32},{64,48},{80,64},{96,80},{112,96},{1... | collective-permute-start | bytes 258056 | tf_op jit(solution)/shard_map/ppermute | solution.py:508
  108.4 3.3 %collective-permute-start.24 = (f32[7,8,384]{2,1,0:T(8,128)S(1)}, f32[7,8,384]{2,1,0:T(8,128)S(1)}, u32[]{:S(2)}, u32[]{:S(2)}) collective-permute-start(f32[7,8,384]{2,1,0:T(8,128)S(1)} %collective-permute-done.21.refs_7_), channel_id=1, source_target_pairs={{0,1},{1,0},{2,3},{3,2},{4,5},{5,4},{6,7},{7,6},{8,9},{9,8},{10,11... | collective-permute-start | bytes 258056 | tf_op jit(solution)/shard_map/ppermute | solution.py:512
  110.8 2.2 %collective-permute-start.19 = (f32[7,8,640]{2,1,0:T(8,128)S(1)}, f32[7,8,640]{2,1,0:T(8,128)S(1)}, u32[]{:S(2)}, u32[]{:S(2)}) collective-permute-start(f32[7,8,640]{2,1,0:T(8,128)S(1)} %collective-permute-done.16.refs_1_), channel_id=1, source_target_pairs={{0,1},{1,0},{2,3},{3,2},{4,5},{5,4},{6,7},{7,6},{8,9},{9,8},{10,11... | collective-permute-start | bytes 430088 | tf_op jit(solution)/shard_map/ppermute | solution.py:512
  110.9 2.1 %collective-permute-start.20 = (f32[7,8,640]{2,1,0:T(8,128)S(1)}, f32[7,8,640]{2,1,0:T(8,128)S(1)}, u32[]{:S(2)}, u32[]{:S(2)}) collective-permute-start(f32[7,8,640]{2,1,0:T(8,128)S(1)} %collective-permute-done.17.refs_2_), channel_id=1, source_target_pairs={{0,1},{1,0},{2,3},{3,2},{4,5},{5,4},{6,7},{7,6},{8,9},{9,8},{10,11... | collective-permute-start | bytes 430088 | tf_op jit(solution)/shard_map/ppermute | solution.py:512
  (34 other events, 154.6 us)
